TPU v7x, 1024 devices: a whole 4x8x16 slice. The times are simulated.
1024 devices in a mesh: blk: 32 (over z, core), row: 8 (over y), depth: 4 (over x).
Axes of the slice: x: 4, y: 8, z: 16, core: 2. Of those that a mesh axis runs over, the one named last changes fastest.
Arguments:
- x_start: bfloat16 [4096, 4096], P('blk', ('row', 'depth')), as said below
- keep_mask: int32 [2, 2, 64, 64], P(None, None, 'blk', ('row', 'depth')), may hold values from 0 to 1, as said below
Outputs:
- sign_estimate: bfloat16 [4096, 4096], P('blk', ('row', 'depth'))
Inputs may be any that keep to these rules, and one draw needn't show every extreme that they name: Each pattern is symmetric (keep_mask[t, s, i, j] = keep_mask[t, s, j, i]) and keeps every diagonal block. x_start is exactly symmetric.
All inputs are finite; a program needn't handle non-finite values.
Results may differ from a plain program's by a relative error of at most 0.0036.
Values may be sent and summed in bfloat16 or wider, within the bound.
No kernel may reach another device: no remote copies, remote signals or barrier semaphores. Data moves between devices by JAX's collectives and lax.ppermute only.
A program may use at most 32 MiB of HBM per device.

v0:
```python
import jax
import jax.numpy as jnp
from jax import lax
from jax.sharding import PartitionSpec as P

BS = 64
ITERS = 2


def expand_blocks(pattern):
    return jnp.repeat(jnp.repeat(pattern, BS, axis=0), BS, axis=1)


def column_cube(add_product, square, empty_tile):
    return add_product(empty_tile, lax.all_gather(square, "blk", axis=0, tiled=True), jnp.int32(0))


def make_adder(row_slab):

    def add_product(running, tile_in, offset):
        return jnp.dot(row_slab, tile_in, preferred_element_type=jnp.float32)

    return add_product


def on_device(x_start, keep_mask):
    current = x_start
    rows_here, cols_here = current.shape
    for step_index in range(ITERS):
        keep_square = expand_blocks(keep_mask[step_index, 0]) == 1
        keep_update = expand_blocks(keep_mask[step_index, 1]) == 1
        row_slab = lax.all_gather(current, ("row", "depth"), axis=1, tiled=True)
        add_product = make_adder(row_slab)
        empty_tile = jnp.zeros((rows_here, cols_here), jnp.float32)
        summed = add_product(
            empty_tile, lax.all_gather(current, "blk", axis=0, tiled=True), jnp.int32(0)
        )
        square = jnp.where(keep_square, summed, jnp.float32(0.0)).astype(jnp.bfloat16)
        if step_index == 0:
            cube_term = column_cube(add_product, square, empty_tile)
        else:
            cube_term = column_cube(add_product, square, empty_tile)
        update = 1.5 * current.astype(jnp.float32) - 0.5 * cube_term
        current = jnp.where(keep_update, update, jnp.float32(0.0)).astype(jnp.bfloat16)
    return current


def solution(mesh):
    return jax.shard_map(
        on_device,
        mesh=mesh,
        in_specs=(P("blk", ("row", "depth")), P(None, None, "blk", ("row", "depth"))),
        out_specs=P("blk", ("row", "depth")),
        check_vma=False,
    )
```

profile of v0, /device:TPU:1, one launch (start us, length us, event | category | flops | bytes accessed | tf_op | source)
XLA Modules:
  0.0 505.6 jit_solution(8471283082192349376)
XLA Ops:
  6.5 0.0 all-gather.7.cloned.1.call-start
  6.5 0.7 all-gather.7.cloned.1.call-update
  7.3 0.0 copy-start.4
  7.3 0.0 all-gather.9.cloned.1.call-start
  7.3 0.7 all-gather.9.cloned.1.call-update
  8.0 0.0 all-gather.11.cloned.1.call-start
  8.1 0.0 copy-done.4
  8.1 0.1 copy.6
  8.2 0.1 broadcast_in_dim.35
  8.3 0.1 eq.66
  8.4 94.9 %all-gather.7.cloned.1.call-done = bf16[128,4096]{1,0:T(8,128)(2,1)} async-done(((bf16[128,128]{1,0:T(8,128)(2,1)}), bf16[128,4096]{1,0:T(8,128)(2,1)}) %all-gather.7.cloned.1.call-update) | async-done | bytes 1048592 | tf_op jit(solution)/shard_map/all_gather | solution.py:32
  103.3 81.3 %all-gather.9.cloned.1.call-done = bf16[4096,128]{1,0:T(8,128)(2,1)} async-done(((bf16[128,128]{1,0:T(8,128)(2,1)}), bf16[4096,128]{1,0:T(8,128)(2,1)}) %all-gather.9.cloned.1.call-update) | async-done | bytes 1048592 | tf_op jit(solution)/shard_map/all_gather | solution.py:36
  184.5 0.0 copy-start
  184.5 2.8 fusion.5
  187.3 0.0 copy-start.3
  187.3 0.0 all-gather.11.cloned.1.call-update
  187.3 0.0 all-gather.13.cloned.1.call-start
  187.4 0.7 copy-done.3
  188.1 0.1 copy.5
  188.2 0.1 copy.4
  188.3 0.1 broadcast_in_dim.33
  188.4 0.1 eq.62
  188.5 69.4 %all-gather.11.cloned.1.call-done = bf16[4096,128]{0,1:T(8,128)(2,1)} async-done(((bf16[128,128]{0,1:T(8,128)(2,1)}), bf16[4096,128]{0,1:T(8,128)(2,1)}) %all-gather.11.cloned.1.call-update) | async-done | bytes 1048592 | tf_op jit(solution)/shard_map/all_gather | solution.py:15
  257.8 0.0 copy-done
  257.8 2.3 fusion.8
  260.1 0.0 all-gather.13.cloned.1.call-update
  260.2 0.0 all-gather.15.cloned.1.call-start
  260.2 0.5 all-gather.15.cloned.1.call-update
  260.7 0.0 all-gather.17.cloned.1.call-start
  260.8 0.1 copy.8
  260.9 0.1 broadcast_in_dim.38
  261.0 0.1 eq.70
  261.1 83.9 %all-gather.13.cloned.1.call-done = bf16[128,4096]{0,1:T(8,128)(2,1)} async-done(((bf16[128,128]{0,1:T(8,128)(2,1)}), bf16[128,4096]{0,1:T(8,128)(2,1)}) %all-gather.13.cloned.1.call-update) | async-done | bytes 1048592 | tf_op jit(solution)/shard_map/all_gather | solution.py:32
  344.9 79.3 %all-gather.15.cloned.1.call-done = bf16[4096,128]{0,1:T(8,128)(2,1)} async-done(((bf16[128,128]{0,1:T(8,128)(2,1)}), bf16[4096,128]{0,1:T(8,128)(2,1)}) %all-gather.15.cloned.1.call-update) | async-done | bytes 1048592 | tf_op jit(solution)/shard_map/all_gather | solution.py:36
  424.3 0.0 copy-start.1
  424.3 2.7 fusion.6
  426.9 0.0 copy-start.2
  426.9 0.0 all-gather.17.cloned.1.call-update
  427.0 0.1 copy.3
  427.1 0.1 broadcast_in_dim.31
  427.2 0.1 eq.58
  427.2 69.1 %all-gather.17.cloned.1.call-done = bf16[4096,128]{0,1:T(8,128)(2,1)} async-done(((bf16[128,128]{0,1:T(8,128)(2,1)}), bf16[4096,128]{0,1:T(8,128)(2,1)}) %all-gather.17.cloned.1.call-update) | async-done | bytes 1048592 | tf_op jit(solution)/shard_map/all_gather | solution.py:15
  496.3 0.0 copy-done.1
  496.3 0.0 copy-done.2
  496.3 1.6 fusion.7
  498.0 0.7 copy.10
  (5 shorter events, 0.0 us)
Async XLA Ops:
  6.5 96.7 %all-gather.7.cloned.1.call-start = ((), (), s32[]{:S(2)}) async-start(), calls=%async_computation | async-start | bytes 1081344 | tf_op jit(solution)/shard_map/all_gather | solution.py:32
  7.3 0.8 copy-start.4
  7.3 177.3 %all-gather.9.cloned.1.call-start = ((), (), s32[]{:S(2)}) async-start(), calls=%async_computation.1 | async-start | bytes 1081344 | tf_op jit(solution)/shard_map/all_gather | solution.py:36
  8.0 249.8 %all-gather.11.cloned.1.call-start = ((), (), s32[]{:S(2)}) async-start(), calls=%async_computation.2 | async-start | bytes 1081344 | tf_op jit(solution)/shard_map/all_gather | solution.py:15
  184.5 73.3 %copy-start = (bf16[128,4096]{1,0:T(8,128)(2,1)S(1)}, bf16[128,4096]{1,0:T(8,128)(2,1)}, u32[]{:S(2)}) copy-start(bf16[128,4096]{1,0:T(8,128)(2,1)} %all-gather.7.cloned.1.call-done) | copy-start | bytes 3145732
  187.3 0.8 copy-start.3
  187.3 157.6 %all-gather.13.cloned.1.call-start = ((), (), s32[]{:S(2)}) async-start(), calls=%async_computation.3 | async-start | bytes 1081344 | tf_op jit(solution)/shard_map/all_gather | solution.py:32
  260.2 164.1 %all-gather.15.cloned.1.call-start = ((), (), s32[]{:S(2)}) async-start(), calls=%async_computation.4 | async-start | bytes 1081344 | tf_op jit(solution)/shard_map/all_gather | solution.py:36
  260.7 235.6 %all-gather.17.cloned.1.call-start = ((), (), s32[]{:S(2)}) async-start(), calls=%async_computation.5 | async-start | bytes 1081344 | tf_op jit(solution)/shard_map/all_gather | solution.py:15
  424.3 72.1 %copy-start.1 = (bf16[128,4096]{0,1:T(8,128)(2,1)S(1)}, bf16[128,4096]{0,1:T(8,128)(2,1)}, u32[]{:S(2)}) copy-start(bf16[128,4096]{0,1:T(8,128)(2,1)} %all-gather.13.cloned.1.call-done) | copy-start | bytes 3145732
  426.9 69.4 %copy-start.2 = (bf16[128,128]{0,1:T(8,128)(2,1)S(1)}, bf16[128,128]{0,1:T(8,128)(2,1)}, u32[]{:S(2)}) copy-start(bf16[128,128]{0,1:T(8,128)(2,1)} %fusion.8) | copy-start | bytes 98308
Sparse Core Ops, SparseCore 0:
  11.6 91.6 all-gather.6
  106.0 78.5 all-gather.8
  187.5 70.3 all-gather.10
  262.0 82.8 all-gather.12
  347.4 76.8 all-gather.14
  427.1 69.1 all-gather.16
where the time goes:
time: 506 us
  waiting for transfers between devices  480 us (95%)
  between operations  13.5 us (3%)
  matrix products  9.36 us (2%)
    all_gather x2, waiting for transfers between devices, on_device(): row_slab = lax.all_gather(current, ('row', 'depth'), axis=1, tiled=True)  179 us
    all_gather x2, waiting for transfers between devices, on_device(): lax.all_gather(current, 'blk', axis=0, tiled=True)  161 us
    all_gather x2, waiting for transfers between devices, column_cube(): lax.all_gather(square, 'blk', axis=0, tiled=True)  138 us
  transfers between devices with their start and end apart: 6, of which 6 were waited for; matrix products, arithmetic and copies ran while one was open for 0% of the time, Pallas kernels for 0%

commit v1 on v0

v1 whole, which is shorter than its diff:
```python
import functools

import jax
import jax.numpy as jnp
from jax import lax
from jax.experimental import pallas as pl
from jax.experimental.pallas import tpu as pltpu
from jax.sharding import Mesh, PartitionSpec as P

BS = 64
ITERS = 2
CORES = 2
LINE = ("z",)
PLANE = ("row", "depth")
ALL = ("z", "core", "row", "depth")
F32 = jnp.float32
BF16 = jnp.bfloat16


def filtered(value, mask_ref):
    block_row = lax.broadcasted_iota(jnp.int32, value.shape, 0) // BS
    block_col = lax.broadcasted_iota(jnp.int32, value.shape, 1) // BS
    keep = jnp.zeros(value.shape, jnp.int32)
    for i in range(value.shape[0] // BS):
        for j in range(value.shape[1] // BS):
            here = jnp.logical_and(block_row == i, block_col == j)
            keep = jnp.where(here, mask_ref[i, j], keep)
    return jnp.where(keep == 1, value, 0.0).astype(BF16)


def slab_product(core_ref, rows_ref, own_ref, other_ref):
    chips, side, cols = own_ref.shape
    core = core_ref[0]
    total = None
    for col_ref, which in ((own_ref, core), (other_ref, 1 - core)):
        left = jnp.concatenate([rows_ref[2 * z + which] for z in range(chips)], axis=1)
        right = col_ref[...].reshape(chips * side, cols)
        term = jnp.dot(left, right, preferred_element_type=F32)
        total = term if total is None else total + term
    return total


def square_kernel(core_ref, mask_ref, rows_ref, own_ref, other_ref, copies_ref):
    tile = filtered(slab_product(core_ref, rows_ref, own_ref, other_ref), mask_ref)
    for i in range(copies_ref.shape[0]):
        copies_ref[i] = tile


def updated(core_ref, mask_ref, rows_ref, own_ref, other_ref, tile_ref):
    cube_term = slab_product(core_ref, rows_ref, own_ref, other_ref)
    return filtered(1.5 * tile_ref[...].astype(F32) - 0.5 * cube_term, mask_ref)


def update_kernel(core_ref, mask_ref, rows_ref, own_ref, other_ref, tile_ref, out_ref, copies_ref):
    tile = updated(core_ref, mask_ref, rows_ref, own_ref, other_ref, tile_ref)
    out_ref[...] = tile
    for i in range(copies_ref.shape[0]):
        copies_ref[i] = tile


def last_kernel(core_ref, mask_ref, rows_ref, own_ref, other_ref, tile_ref, out_ref):
    tile = updated(core_ref, mask_ref, rows_ref, own_ref, other_ref, tile_ref)
    out_ref[...] = tile.astype(F32).T.astype(BF16)


def call(kernel, scalars, arrays, outs):
    smem = pl.BlockSpec(memory_space=pltpu.SMEM)
    vmem = pl.BlockSpec(memory_space=pltpu.VMEM)
    return pl.pallas_call(
        kernel,
        out_shape=[jax.ShapeDtypeStruct(shape, BF16) for shape in outs],
        in_specs=[smem] * len(scalars) + [vmem] * len(arrays),
        out_specs=[vmem] * len(outs),
        compiler_params=pltpu.CompilerParams(vmem_limit_bytes=32 << 20),
    )(*scalars, *arrays)


def on_device(x_start, keep_mask):
    side = x_start.shape[0]
    tiles = lax.axis_size(PLANE)
    blk = lax.axis_size(LINE) * CORES
    core = lax.axis_index("core").astype(jnp.int32).reshape(1)
    tile, copies = x_start, jnp.broadcast_to(x_start[None], (tiles, side, side))
    for step in range(ITERS):
        rows = lax.all_to_all(copies, PLANE, 0, 0)
        own = lax.all_gather(tile, LINE, axis=0)
        other = lax.ppermute(own, "core", [(0, 1), (1, 0)])
        (copies,) = call(
            square_kernel, [core, keep_mask[step, 0]], [rows, own, other], [(tiles, side, side)]
        )
        rows = lax.all_to_all(copies, PLANE, 0, 0)
        scalars, arrays = [core, keep_mask[step, 1]], [rows, own, other, tile]
        if step < ITERS - 1:
            tile, copies = call(
                update_kernel, scalars, arrays, [(side, side), (tiles, side, side)]
            )
        else:
            (tile,) = call(last_kernel, scalars, arrays, [(side, side)])
    swap = [(b * tiles + c, c * tiles + b) for b in range(blk) for c in range(tiles)]
    return lax.ppermute(tile, ALL, swap)


def solution(mesh):
    blk, row, depth = mesh.devices.shape
    fine = Mesh(mesh.devices.reshape(blk // CORES, CORES, row, depth), ALL)
    spec = P(("z", "core"), PLANE)
    return jax.shard_map(
        on_device,
        mesh=fine,
        in_specs=(spec, P(None, None, ("z", "core"), PLANE)),
        out_specs=spec,
        check_vma=False,
    )
```

time: 506 us -> 199 us (0.39)
  the two profiles are of different devices: /device:TPU:1 before, /device:TPU:96 now
where the time goes in v1:
time: 199 us; the launch traced here: 198 us
  blocking collectives  143 us (72%)
  starting transfers between devices  32 us (16%)
  waiting for transfers between devices  15.1 us (8%)
  Pallas kernels  5.22 us (3%)
  local copies, waits for them, and re-layouts  2.59 us (1%)
    all_gather x2, blocking collectives, on_device(): own = lax.all_gather(tile, LINE, axis=0)  73.6 us
    all_to_all x2, blocking collectives, on_device(): rows = lax.all_to_all(copies, PLANE, 0, 0)  69.8 us
    all_to_all x2, starting transfers between devices, on_device(): rows = lax.all_to_all(copies, PLANE, 0, 0)  18.5 us
    ppermute x1, waiting for transfers between devices, on_device(): return lax.ppermute(tile, ALL, swap)  11.3 us
    ppermute x1, starting transfers between devices, on_device(): return lax.ppermute(tile, ALL, swap)  9.53 us
    pallas_call x4, Pallas kernels, call(): pl.pallas_call(kernel, out_shape=[jax.ShapeDtypeStruct(shape, BF16) for s...  5.22 us
  transfers between devices with their start and end apart: 5, of which 3 were waited for; matrix products, arithmetic and copies ran while one was open for 0% of the time, Pallas kernels for 0%

profile of v1, /device:TPU:96, one launch (start us, length us, event | category | flops | bytes accessed | tf_op | source)
XLA Modules:
  0.0 198.4 jit_solution(1702284626611242981)
XLA Ops:
  0.0 2.0 broadcast_in_dim.8
  2.0 0.0 copy-start
  2.0 10.0 %all-to-all-start = ((bf16[32,128,128]{2,1,0:T(8,128)(2,1)}), bf16[32,128,128]{2,1,0:T(8,128)(2,1)S(1)}, u32[]{:S(2)}, u32[]{:S(2)}) async-start(bf16[32,128,128]{2,1,0:T(8,128)(2,1)} %broadcast_in_dim.8), calls=%async_computation | async-start | bytes 2097152 | tf_op jit(solution)/shard_map/all_to_all | solution.py:85
  11.9 0.0 copy-done
  12.0 42.1 %all-gather = bf16[2048,128]{1,0:T(8,128)(2,1)S(1)} all-gather(bf16[128,128]{1,0:T(8,128)(2,1)S(1)} %copy-done), channel_id=2, replica_groups=mesh['z'=16,'core'=2,'row'=8,'depth'=4] {'z'}, dimensions={0}, use_global_device_ids=true | all-gather | bytes 557056 | tf_op jit(solution)/shard_map/all_gather | solution.py:86
  54.1 0.0 copy-start.1
  54.1 2.0 %collective-permute-start = (bf16[16,128,128]{2,1,0:T(8,128)(2,1)S(1)}, bf16[16,128,128]{2,1,0:T(8,128)(2,1)S(1)}, u32[]{:S(2)}, u32[]{:S(2)}) collective-permute-start(bf16[16,128,128]{2,1,0:T(8,128)(2,1)S(1)} %bitcast.14), channel_id=1, source_target_pairs={{0,32},{32,0},{1,33},{33,1},{2,34},{34,2},{3,35},{35,3},{4,36},{36... | collective-permute-start | bytes 1572872 | tf_op jit(solution)/shard_map/ppermute | solution.py:87
  56.1 0.0 copy-done.1
  56.1 1.8 collective-permute-done.other_ref
  58.0 0.0 all-to-all-done.rows_ref
  58.0 1.1 shard_map.28
  59.1 34.9 %all_to_all.20.rows_ref = bf16[32,128,128]{2,1,0:T(8,128)(2,1)S(1)} all-to-all(bf16[32,128,128]{2,1,0:T(8,128)(2,1)S(1)} %shard_map.28), channel_id=1, replica_groups=mesh['z'=16,'core'=2,'row'=8,'depth'=4] {'row','depth'}, dimensions={0} | all-to-all | bytes 2097152 | tf_op jit(solution)/shard_map/all_to_all | solution.py:91
  93.9 2.1 %shard_map.29 = (bf16[128,128]{1,0:T(8,128)(2,1)S(1)}, bf16[32,128,128]{2,1,0:T(8,128)(2,1)}) custom-call(s32[1]{0:T(128)} %bitcast.core_ref, s32[2,2]{1,0:T(2,128)S(1)} %get-tuple-element.12.mask_ref, bf16[32,128,128]{2,1,0:T(8,128)(2,1)S(1)} %all_to_all.20.rows_ref, bf16[16,128,128]{2,1,0:T(8,128)(2,1)S(1)} %bitcast.16, ...), custom_call_target="tpu_custom_call" | custom-call | tf_op jit(solution)/shard_map/pallas_call | solution.py:69
  96.0 8.6 %all-to-all-start.2 = ((bf16[32,128,128]{2,1,0:T(8,128)(2,1)}), bf16[32,128,128]{2,1,0:T(8,128)(2,1)S(1)}, u32[]{:S(2)}, u32[]{:S(2)}) async-start(bf16[32,128,128]{2,1,0:T(8,128)(2,1)} %get-tuple-element.7), calls=%async_computation.2 | async-start | bytes 2097152 | tf_op jit(solution)/shard_map/all_to_all | solution.py:85
  104.6 31.5 %all-gather.1 = bf16[2048,128]{1,0:T(8,128)(2,1)S(1)} all-gather(bf16[128,128]{1,0:T(8,128)(2,1)S(1)} %get-tuple-element.8.tile_ref), channel_id=3, replica_groups=mesh['z'=16,'core'=2,'row'=8,'depth'=4] {'z'}, dimensions={0}, use_global_device_ids=true | all-gather | bytes 557056 | tf_op jit(solution)/shard_map/all_gather | solution.py:86
  136.1 1.9 collective-permute-start.1
  138.0 1.9 collective-permute-done.1.other_ref
  139.9 0.0 all-to-all-done.2.rows_ref
  139.9 1.1 shard_map.30
  141.0 34.9 %all_to_all.21.rows_ref = bf16[32,128,128]{2,1,0:T(8,128)(2,1)S(1)} all-to-all(bf16[32,128,128]{2,1,0:T(8,128)(2,1)S(1)} %shard_map.30), channel_id=1, replica_groups=mesh['z'=16,'core'=2,'row'=8,'depth'=4] {'row','depth'}, dimensions={0} | all-to-all | bytes 2097152 | tf_op jit(solution)/shard_map/all_to_all | solution.py:91
  175.9 1.1 shard_map.31
  177.0 9.5 %collective-permute-start.2 = (bf16[128,128]{1,0:T(8,128)(2,1)S(1)}, bf16[128,128]{1,0:T(8,128)(2,1)S(1)}, u32[]{:S(2)}, u32[]{:S(2)}) collective-permute-start(bf16[128,128]{1,0:T(8,128)(2,1)S(1)} %shard_map.31), channel_id=1, source_target_pairs={{0,0},{1,32},{2,64},{3,96},{4,128},{5,160},{6,192},{7,224},{8,256}... | collective-permute-start | bytes 98312 | tf_op jit(solution)/shard_map/ppermute | solution.py:100
  186.5 11.3 %collective-permute-done.2 = bf16[128,128]{1,0:T(8,128)(2,1)S(1)} collective-permute-done((bf16[128,128]{1,0:T(8,128)(2,1)S(1)}, bf16[128,128]{1,0:T(8,128)(2,1)S(1)}, u32[]{:S(2)}, u32[]{:S(2)}) %collective-permute-start.2) | collective-permute-done | bytes 32800 | tf_op jit(solution)/shard_map/ppermute | solution.py:100
  197.8 0.6 copy.4
  (1 shorter events, 0.0 us)
Async XLA Ops:
  2.0 10.0 %copy-start = (bf16[128,128]{1,0:T(8,128)(2,1)S(1)}, bf16[128,128]{1,0:T(8,128)(2,1)}, u32[]{:S(2)}) copy-start(bf16[128,128]{1,0:T(8,128)(2,1)} %tile_ref.1) | copy-start | bytes 98308
  2.0 56.0 %all-to-all-start = ((bf16[32,128,128]{2,1,0:T(8,128)(2,1)}), bf16[32,128,128]{2,1,0:T(8,128)(2,1)S(1)}, u32[]{:S(2)}, u32[]{:S(2)}) async-start(bf16[32,128,128]{2,1,0:T(8,128)(2,1)} %broadcast_in_dim.8), calls=%async_computation | async-start | bytes 2097152 | tf_op jit(solution)/shard_map/all_to_all | solution.py:85
  54.1 2.1 %copy-start.1 = (s32[2,2,2,2]{3,2,1,0:T(2,128)S(1)}, s32[2,2,2,2]{3,2,1,0:T(2,128)}, u32[]{:S(2)}) copy-start(s32[2,2,2,2]{3,2,1,0:T(2,128)} %param.3) | copy-start | bytes 196
  54.1 3.9 %collective-permute-start = (bf16[16,128,128]{2,1,0:T(8,128)(2,1)S(1)}, bf16[16,128,128]{2,1,0:T(8,128)(2,1)S(1)}, u32[]{:S(2)}, u32[]{:S(2)}) collective-permute-start(bf16[16,128,128]{2,1,0:T(8,128)(2,1)S(1)} %bitcast.14), channel_id=1, source_target_pairs={{0,32},{32,0},{1,33},{33,1},{2,34},{34,2},{3,35},{35,3},{4,36},{36... | collective-permute-start | bytes 1572872 | tf_op jit(solution)/shard_map/ppermute | solution.py:87
  96.0 43.9 %all-to-all-start.2 = ((bf16[32,128,128]{2,1,0:T(8,128)(2,1)}), bf16[32,128,128]{2,1,0:T(8,128)(2,1)S(1)}, u32[]{:S(2)}, u32[]{:S(2)}) async-start(bf16[32,128,128]{2,1,0:T(8,128)(2,1)} %get-tuple-element.7), calls=%async_computation.2 | async-start | bytes 2097152 | tf_op jit(solution)/shard_map/all_to_all | solution.py:85
  136.1 3.8 %collective-permute-start.1 = (bf16[16,128,128]{2,1,0:T(8,128)(2,1)S(1)}, bf16[16,128,128]{2,1,0:T(8,128)(2,1)S(1)}, u32[]{:S(2)}, u32[]{:S(2)}) collective-permute-start(bf16[16,128,128]{2,1,0:T(8,128)(2,1)S(1)} %bitcast.11), channel_id=1, source_target_pairs={{0,32},{32,0},{1,33},{33,1},{2,34},{34,2},{3,35},{35,3},{4,36},{36... | collective-permute-start | bytes 1572872 | tf_op jit(solution)/shard_map/ppermute | solution.py:87
  177.0 20.9 %collective-permute-start.2 = (bf16[128,128]{1,0:T(8,128)(2,1)S(1)}, bf16[128,128]{1,0:T(8,128)(2,1)S(1)}, u32[]{:S(2)}, u32[]{:S(2)}) collective-permute-start(bf16[128,128]{1,0:T(8,128)(2,1)S(1)} %shard_map.31), channel_id=1, source_target_pairs={{0,0},{1,32},{2,64},{3,96},{4,128},{5,160},{6,192},{7,224},{8,256}... | collective-permute-start | bytes 98312 | tf_op jit(solution)/shard_map/ppermute | solution.py:100

commit v2 on v1

--- a/solution.py
+++ b/solution.py
@@ -1,5 +1,3 @@
-import functools
-
 import jax
 import jax.numpy as jnp
 from jax import lax
@@ -40,27 +38,17 @@
     return total
 
 
-def square_kernel(core_ref, mask_ref, rows_ref, own_ref, other_ref, copies_ref):
-    tile = filtered(slab_product(core_ref, rows_ref, own_ref, other_ref), mask_ref)
-    for i in range(copies_ref.shape[0]):
-        copies_ref[i] = tile
+def square_kernel(core_ref, mask_ref, rows_ref, own_ref, other_ref, out_ref):
+    out_ref[...] = filtered(slab_product(core_ref, rows_ref, own_ref, other_ref), mask_ref)
 
 
-def updated(core_ref, mask_ref, rows_ref, own_ref, other_ref, tile_ref):
+def update_kernel(core_ref, mask_ref, rows_ref, own_ref, other_ref, tile_ref, out_ref, *copies_refs):
     cube_term = slab_product(core_ref, rows_ref, own_ref, other_ref)
-    return filtered(1.5 * tile_ref[...].astype(F32) - 0.5 * cube_term, mask_ref)
-
-
-def update_kernel(core_ref, mask_ref, rows_ref, own_ref, other_ref, tile_ref, out_ref, copies_ref):
-    tile = updated(core_ref, mask_ref, rows_ref, own_ref, other_ref, tile_ref)
+    tile = filtered(1.5 * tile_ref[...].astype(F32) - 0.5 * cube_term, mask_ref)
     out_ref[...] = tile
-    for i in range(copies_ref.shape[0]):
-        copies_ref[i] = tile
-
-
-def last_kernel(core_ref, mask_ref, rows_ref, own_ref, other_ref, tile_ref, out_ref):
-    tile = updated(core_ref, mask_ref, rows_ref, own_ref, other_ref, tile_ref)
-    out_ref[...] = tile.astype(F32).T.astype(BF16)
+    for copies_ref in copies_refs:
+        for i in range(copies_ref.shape[0]):
+            copies_ref[i] = tile
 
 
 def call(kernel, scalars, arrays, outs):
@@ -75,29 +63,27 @@
     )(*scalars, *arrays)
 
 
+def column_slab(tile):
+    own = lax.all_gather(tile, LINE, axis=0)
+    return own, lax.ppermute(own, "core", [(0, 1), (1, 0)])
+
+
 def on_device(x_start, keep_mask):
     side = x_start.shape[0]
     tiles = lax.axis_size(PLANE)
-    blk = lax.axis_size(LINE) * CORES
     core = lax.axis_index("core").astype(jnp.int32).reshape(1)
     tile, copies = x_start, jnp.broadcast_to(x_start[None], (tiles, side, side))
     for step in range(ITERS):
         rows = lax.all_to_all(copies, PLANE, 0, 0)
-        own = lax.all_gather(tile, LINE, axis=0)
-        other = lax.ppermute(own, "core", [(0, 1), (1, 0)])
-        (copies,) = call(
-            square_kernel, [core, keep_mask[step, 0]], [rows, own, other], [(tiles, side, side)]
+        (square,) = call(
+            square_kernel, [core, keep_mask[step, 0]], [rows, *column_slab(tile)], [(side, side)]
         )
-        rows = lax.all_to_all(copies, PLANE, 0, 0)
-        scalars, arrays = [core, keep_mask[step, 1]], [rows, own, other, tile]
-        if step < ITERS - 1:
-            tile, copies = call(
-                update_kernel, scalars, arrays, [(side, side), (tiles, side, side)]
-            )
-        else:
-            (tile,) = call(last_kernel, scalars, arrays, [(side, side)])
-    swap = [(b * tiles + c, c * tiles + b) for b in range(blk) for c in range(tiles)]
-    return lax.ppermute(tile, ALL, swap)
+        outs = [(side, side)] + [(tiles, side, side)] * (step < ITERS - 1)
+        tile, *copies = call(
+            update_kernel, [core, keep_mask[step, 1]], [rows, *column_slab(square), tile], outs
+        )
+        copies = copies[0] if copies else None
+    return tile
 
 
 def solution(mesh):

time: 199 us -> 179 us (0.90)
  the two profiles are of different devices: /device:TPU:96 before, /device:TPU:1 now
where the time goes in v2:
time: 179 us; the launch traced here: 178 us
  blocking collectives  110 us (61%)
  starting transfers between devices  54.4 us (30%)
  waiting for transfers between devices  6.04 us (3%)
  Pallas kernels  5.65 us (3%)
  local copies, waits for them, and re-layouts  1.98 us (1%)
    all_gather x4, blocking collectives, column_slab(): own = lax.all_gather(tile, LINE, axis=0)  110 us
    ppermute x4, starting transfers between devices, column_slab(): return (own, lax.ppermute(own, 'core', [(0, 1), (1, 0)]))  34.1 us
    all_to_all x2, starting transfers between devices, on_device(): rows = lax.all_to_all(copies, PLANE, 0, 0)  20.3 us
    ppermute x4, waiting for transfers between devices, column_slab(): return (own, lax.ppermute(own, 'core', [(0, 1), (1, 0)]))  6.03 us
    pallas_call x4, Pallas kernels, call(): pl.pallas_call(kernel, out_shape=[jax.ShapeDtypeStruct(shape, BF16) for s...  5.65 us
  transfers between devices with their start and end apart: 6, of which 4 were waited for; matrix products, arithmetic and copies ran while one was open for 0% of the time, Pallas kernels for 0%

profile of v2, /device:TPU:1, one launch (start us, length us, event | category | flops | bytes accessed | tf_op | source)
XLA Modules:
  0.0 178.1 jit_solution(16753508369530802041)
XLA Ops:
  0.0 2.0 %broadcast_in_dim.8 = bf16[32,128,128]{2,1,0:T(8,128)(2,1)} broadcast(bf16[128,128]{1,0:T(8,128)(2,1)} %tile_ref.1), dimensions={1,2} | broadcast | bytes 1081344 | tf_op jit(solution)/shard_map/broadcast_in_dim | solution.py:75
  2.0 0.0 copy-start
  2.0 10.6 %all-to-all-start = ((bf16[32,128,128]{2,1,0:T(8,128)(2,1)}), bf16[32,128,128]{2,1,0:T(8,128)(2,1)S(1)}, u32[]{:S(2)}, u32[]{:S(2)}) async-start(bf16[32,128,128]{2,1,0:T(8,128)(2,1)} %broadcast_in_dim.8), calls=%async_computation | async-start | bytes 2097152 | tf_op jit(solution)/shard_map/all_to_all | solution.py:77
  12.6 0.0 copy-done
  12.6 39.9 %all-gather = bf16[2048,128]{1,0:T(8,128)(2,1)S(1)} all-gather(bf16[128,128]{1,0:T(8,128)(2,1)S(1)} %copy-done), channel_id=2, replica_groups=mesh['z'=16,'core'=2,'row'=8,'depth'=4] {'z'}, dimensions={0}, use_global_device_ids=true | all-gather | bytes 557056 | tf_op jit(solution)/shard_map/all_gather | solution.py:67
  52.5 0.0 copy-start.1
  52.5 8.1 %collective-permute-start = (bf16[16,128,128]{2,1,0:T(8,128)(2,1)S(1)}, bf16[16,128,128]{2,1,0:T(8,128)(2,1)S(1)}, u32[]{:S(2)}, u32[]{:S(2)}) collective-permute-start(bf16[16,128,128]{2,1,0:T(8,128)(2,1)S(1)} %bitcast.15), channel_id=1, source_target_pairs={{0,32},{32,0},{1,33},{33,1},{2,34},{34,2},{3,35},{35,3},{4,36},{36... | collective-permute-start | bytes 1572872 | tf_op jit(solution)/shard_map/ppermute | solution.py:68
  60.6 0.0 copy-done.1
  60.7 1.5 collective-permute-done.other_ref
  62.1 0.0 all-to-all-done.rows_ref
  62.1 1.0 shard_map.28
  63.1 22.2 %all-gather.1 = bf16[2048,128]{1,0:T(8,128)(2,1)S(1)} all-gather(bf16[128,128]{1,0:T(8,128)(2,1)S(1)} %shard_map.28), channel_id=3, replica_groups=mesh['z'=16,'core'=2,'row'=8,'depth'=4] {'z'}, dimensions={0}, use_global_device_ids=true | all-gather | bytes 557056 | tf_op jit(solution)/shard_map/all_gather | solution.py:67
  85.3 9.3 %collective-permute-start.1 = (bf16[16,128,128]{2,1,0:T(8,128)(2,1)S(1)}, bf16[16,128,128]{2,1,0:T(8,128)(2,1)S(1)}, u32[]{:S(2)}, u32[]{:S(2)}) collective-permute-start(bf16[16,128,128]{2,1,0:T(8,128)(2,1)S(1)} %bitcast.19), channel_id=1, source_target_pairs={{0,32},{32,0},{1,33},{33,1},{2,34},{34,2},{3,35},{35,3},{4,36},{36... | collective-permute-start | bytes 1572872 | tf_op jit(solution)/shard_map/ppermute | solution.py:68
  94.7 1.5 collective-permute-done.1.other_ref
  96.2 2.1 %shard_map.29 = (bf16[128,128]{1,0:T(8,128)(2,1)S(1)}, bf16[32,128,128]{2,1,0:T(8,128)(2,1)}) custom-call(s32[1]{0:T(128)} %bitcast.core_ref, s32[2,2]{1,0:T(2,128)S(1)} %get-tuple-element.10.mask_ref, bf16[32,128,128]{2,1,0:T(8,128)(2,1)S(1)} %all-to-all-done.rows_ref, bf16[16,128,128]{2,1,0:T(8,128)(2,1)S(1)} %bitcast.20, ...), custom_call_target="tpu_custom_call" | custom-call | tf_op jit(solution)/shard_map/pallas_call | solution.py:57
  98.3 9.7 %all-to-all-start.1 = ((bf16[32,128,128]{2,1,0:T(8,128)(2,1)}), bf16[32,128,128]{2,1,0:T(8,128)(2,1)S(1)}, u32[]{:S(2)}, u32[]{:S(2)}) async-start(bf16[32,128,128]{2,1,0:T(8,128)(2,1)} %get-tuple-element.7), calls=%async_computation.1 | async-start | bytes 2097152 | tf_op jit(solution)/shard_map/all_to_all | solution.py:77
  108.0 25.3 %all-gather.2 = bf16[2048,128]{1,0:T(8,128)(2,1)S(1)} all-gather(bf16[128,128]{1,0:T(8,128)(2,1)S(1)} %get-tuple-element.8.tile_ref), channel_id=4, replica_groups=mesh['z'=16,'core'=2,'row'=8,'depth'=4] {'z'}, dimensions={0}, use_global_device_ids=true | all-gather | bytes 557056 | tf_op jit(solution)/shard_map/all_gather | solution.py:67
  133.2 7.6 %collective-permute-start.2 = (bf16[16,128,128]{2,1,0:T(8,128)(2,1)S(1)}, bf16[16,128,128]{2,1,0:T(8,128)(2,1)S(1)}, u32[]{:S(2)}, u32[]{:S(2)}) collective-permute-start(bf16[16,128,128]{2,1,0:T(8,128)(2,1)S(1)} %bitcast.17), channel_id=1, source_target_pairs={{0,32},{32,0},{1,33},{33,1},{2,34},{34,2},{3,35},{35,3},{4,36},{36... | collective-permute-start | bytes 1572872 | tf_op jit(solution)/shard_map/ppermute | solution.py:68
  140.8 1.5 collective-permute-done.2.other_ref
  142.3 0.0 all-to-all-done.1.rows_ref
  142.3 1.0 shard_map.30
  143.3 22.6 %all-gather.3 = bf16[2048,128]{1,0:T(8,128)(2,1)S(1)} all-gather(bf16[128,128]{1,0:T(8,128)(2,1)S(1)} %shard_map.30), channel_id=5, replica_groups=mesh['z'=16,'core'=2,'row'=8,'depth'=4] {'z'}, dimensions={0}, use_global_device_ids=true | all-gather | bytes 557056 | tf_op jit(solution)/shard_map/all_gather | solution.py:67
  165.9 9.1 %collective-permute-start.3 = (bf16[16,128,128]{2,1,0:T(8,128)(2,1)S(1)}, bf16[16,128,128]{2,1,0:T(8,128)(2,1)S(1)}, u32[]{:S(2)}, u32[]{:S(2)}) collective-permute-start(bf16[16,128,128]{2,1,0:T(8,128)(2,1)S(1)} %bitcast.13), channel_id=1, source_target_pairs={{0,32},{32,0},{1,33},{33,1},{2,34},{34,2},{3,35},{35,3},{4,36},{36... | collective-permute-start | bytes 1572872 | tf_op jit(solution)/shard_map/ppermute | solution.py:68
  175.0 1.5 collective-permute-done.3.other_ref
  176.5 1.6 shard_map.31
  (1 shorter events, 0.0 us)
Async XLA Ops:
  2.0 10.6 %copy-start = (bf16[128,128]{1,0:T(8,128)(2,1)S(1)}, bf16[128,128]{1,0:T(8,128)(2,1)}, u32[]{:S(2)}) copy-start(bf16[128,128]{1,0:T(8,128)(2,1)} %tile_ref.1) | copy-start | bytes 98308
  2.0 60.2 %all-to-all-start = ((bf16[32,128,128]{2,1,0:T(8,128)(2,1)}), bf16[32,128,128]{2,1,0:T(8,128)(2,1)S(1)}, u32[]{:S(2)}, u32[]{:S(2)}) async-start(bf16[32,128,128]{2,1,0:T(8,128)(2,1)} %broadcast_in_dim.8), calls=%async_computation | async-start | bytes 2097152 | tf_op jit(solution)/shard_map/all_to_all | solution.py:77
  52.5 8.1 %copy-start.1 = (s32[2,2,2,2]{3,2,1,0:T(2,128)S(1)}, s32[2,2,2,2]{3,2,1,0:T(2,128)}, u32[]{:S(2)}) copy-start(s32[2,2,2,2]{3,2,1,0:T(2,128)} %param.3) | copy-start | bytes 196
  52.5 9.6 %collective-permute-start = (bf16[16,128,128]{2,1,0:T(8,128)(2,1)S(1)}, bf16[16,128,128]{2,1,0:T(8,128)(2,1)S(1)}, u32[]{:S(2)}, u32[]{:S(2)}) collective-permute-start(bf16[16,128,128]{2,1,0:T(8,128)(2,1)S(1)} %bitcast.15), channel_id=1, source_target_pairs={{0,32},{32,0},{1,33},{33,1},{2,34},{34,2},{3,35},{35,3},{4,36},{36... | collective-permute-start | bytes 1572872 | tf_op jit(solution)/shard_map/ppermute | solution.py:68
  85.3 10.8 %collective-permute-start.1 = (bf16[16,128,128]{2,1,0:T(8,128)(2,1)S(1)}, bf16[16,128,128]{2,1,0:T(8,128)(2,1)S(1)}, u32[]{:S(2)}, u32[]{:S(2)}) collective-permute-start(bf16[16,128,128]{2,1,0:T(8,128)(2,1)S(1)} %bitcast.19), channel_id=1, source_target_pairs={{0,32},{32,0},{1,33},{33,1},{2,34},{34,2},{3,35},{35,3},{4,36},{36... | collective-permute-start | bytes 1572872 | tf_op jit(solution)/shard_map/ppermute | solution.py:68
  98.3 44.1 %all-to-all-start.1 = ((bf16[32,128,128]{2,1,0:T(8,128)(2,1)}), bf16[32,128,128]{2,1,0:T(8,128)(2,1)S(1)}, u32[]{:S(2)}, u32[]{:S(2)}) async-start(bf16[32,128,128]{2,1,0:T(8,128)(2,1)} %get-tuple-element.7), calls=%async_computation.1 | async-start | bytes 2097152 | tf_op jit(solution)/shard_map/all_to_all | solution.py:77
  133.2 9.1 %collective-permute-start.2 = (bf16[16,128,128]{2,1,0:T(8,128)(2,1)S(1)}, bf16[16,128,128]{2,1,0:T(8,128)(2,1)S(1)}, u32[]{:S(2)}, u32[]{:S(2)}) collective-permute-start(bf16[16,128,128]{2,1,0:T(8,128)(2,1)S(1)} %bitcast.17), channel_id=1, source_target_pairs={{0,32},{32,0},{1,33},{33,1},{2,34},{34,2},{3,35},{35,3},{4,36},{36... | collective-permute-start | bytes 1572872 | tf_op jit(solution)/shard_map/ppermute | solution.py:68
  165.9 10.6 %collective-permute-start.3 = (bf16[16,128,128]{2,1,0:T(8,128)(2,1)S(1)}, bf16[16,128,128]{2,1,0:T(8,128)(2,1)S(1)}, u32[]{:S(2)}, u32[]{:S(2)}) collective-permute-start(bf16[16,128,128]{2,1,0:T(8,128)(2,1)S(1)} %bitcast.13), channel_id=1, source_target_pairs={{0,32},{32,0},{1,33},{33,1},{2,34},{34,2},{3,35},{35,3},{4,36},{36... | collective-permute-start | bytes 1572872 | tf_op jit(solution)/shard_map/ppermute | solution.py:68

commit v3 on v2

v3 whole, which is shorter than its diff:
```python
import jax
import jax.numpy as jnp
from jax import lax
from jax.experimental import pallas as pl
from jax.experimental.pallas import tpu as pltpu
from jax.sharding import PartitionSpec as P

BS = 64
ITERS = 2
CORES = 2
PLANE = ("row", "depth")
F32 = jnp.float32
BF16 = jnp.bfloat16


def filtered(value, mask_ref):
    block_row = lax.broadcasted_iota(jnp.int32, value.shape, 0) // BS
    block_col = lax.broadcasted_iota(jnp.int32, value.shape, 1) // BS
    keep = jnp.zeros(value.shape, jnp.int32)
    for i in range(value.shape[0] // BS):
        for j in range(value.shape[1] // BS):
            here = jnp.logical_and(block_row == i, block_col == j)
            keep = jnp.where(here, mask_ref[i, j], keep)
    return jnp.where(keep == 1, value, 0.0).astype(BF16)


def slab_product(ring_ref, rows_ref, own_ref, other_ref):
    chips, side, cols = own_ref.shape
    total = None
    for col_ref, ring in ((own_ref, ring_ref[0]), (other_ref, 1 - ring_ref[0])):
        cores = [1 - ring if z % 2 else ring for z in range(chips)]
        left = jnp.concatenate([rows_ref[CORES * z + cores[z]] for z in range(chips)], axis=1)
        right = col_ref[...].reshape(chips * side, cols)
        term = jnp.dot(left, right, preferred_element_type=F32)
        total = term if total is None else total + term
    return total


def square_kernel(ring_ref, mask_ref, rows_ref, own_ref, other_ref, out_ref):
    out_ref[...] = filtered(slab_product(ring_ref, rows_ref, own_ref, other_ref), mask_ref)


def update_kernel(ring_ref, mask_ref, rows_ref, own_ref, other_ref, tile_ref, out_ref, *copies_refs):
    cube_term = slab_product(ring_ref, rows_ref, own_ref, other_ref)
    tile = filtered(1.5 * tile_ref[...].astype(F32) - 0.5 * cube_term, mask_ref)
    out_ref[...] = tile
    for copies_ref in copies_refs:
        for i in range(copies_ref.shape[0]):
            copies_ref[i] = tile


def call(kernel, scalars, arrays, outs):
    smem = pl.BlockSpec(memory_space=pltpu.SMEM)
    vmem = pl.BlockSpec(memory_space=pltpu.VMEM)
    return pl.pallas_call(
        kernel,
        out_shape=[jax.ShapeDtypeStruct(shape, BF16) for shape in outs],
        in_specs=[smem] * len(scalars) + [vmem] * len(arrays),
        out_specs=[vmem] * len(outs),
        compiler_params=pltpu.CompilerParams(vmem_limit_bytes=32 << 20),
    )(*scalars, *arrays)


def column_slab(tile):
    chips = lax.axis_size("blk") // CORES
    rings = [[CORES * z + (z + p) % CORES for z in range(chips)] for p in range(CORES)]
    own = lax.all_gather(tile, "blk", axis=0, axis_index_groups=rings)
    swap = [(CORES * z + k, CORES * z + 1 - k) for z in range(chips) for k in range(CORES)]
    return own, lax.ppermute(own, "blk", swap)


def on_device(x_start, keep_mask):
    side = x_start.shape[0]
    tiles = lax.axis_size(PLANE)
    place = lax.axis_index("blk")
    ring = ((place // CORES + place) % CORES).astype(jnp.int32).reshape(1)
    tile, copies = x_start, jnp.broadcast_to(x_start[None], (tiles, side, side))
    for step in range(ITERS):
        rows = lax.all_to_all(copies, PLANE, 0, 0)
        (square,) = call(
            square_kernel, [ring, keep_mask[step, 0]], [rows, *column_slab(tile)], [(side, side)]
        )
        outs = [(side, side)] + [(tiles, side, side)] * (step < ITERS - 1)
        tile, *copies = call(
            update_kernel, [ring, keep_mask[step, 1]], [rows, *column_slab(square), tile], outs
        )
        copies = copies[0] if copies else None
    return tile


def solution(mesh):
    spec = P("blk", PLANE)
    return jax.shard_map(
        on_device,
        mesh=mesh,
        in_specs=(spec, P(None, None, "blk", PLANE)),
        out_specs=spec,
        check_vma=False,
    )
```

time: 179 us -> 166 us (0.927)
  starting transfers between devices: 54.4 us -> 28.7 us
  blocking collectives: 110 us -> 123 us
    ppermute x4, starting transfers between devices: 34.1 us -> 8.86 us  [column_slab(): return (own, lax.ppermute(own, 'blk', swap))]
    all_gather x4, blocking collectives: 110 us -> 123 us  [column_slab(): own = lax.all_gather(tile, 'blk', axis=0, axis_index_groups=rings)]
where the time goes in v3:
time: 166 us
  blocking collectives  123 us (74%)
  starting transfers between devices  28.7 us (17%)
  Pallas kernels  5.65 us (3%)
  waiting for transfers between devices  5.59 us (3%)
  local copies, waits for them, and re-layouts  2.65 us (2%)
    all_gather x4, blocking collectives, column_slab(): own = lax.all_gather(tile, 'blk', axis=0, axis_index_groups=rings)  123 us
    all_to_all x2, starting transfers between devices, on_device(): rows = lax.all_to_all(copies, PLANE, 0, 0)  19.9 us
    ppermute x4, starting transfers between devices, column_slab(): return (own, lax.ppermute(own, 'blk', swap))  8.86 us
    pallas_call x4, Pallas kernels, call(): pl.pallas_call(kernel, out_shape=[jax.ShapeDtypeStruct(shape, BF16) for s...  5.65 us
    ppermute x4, waiting for transfers between devices, column_slab(): return (own, lax.ppermute(own, 'blk', swap))  5.58 us
  transfers between devices with their start and end apart: 6, of which 4 were waited for; matrix products, arithmetic and copies ran while one was open for 0% of the time, Pallas kernels for 0%

profile of v3, /device:TPU:1, one launch (start us, length us, event | category | flops | bytes accessed | tf_op | source)
XLA Modules:
  0.0 165.7 jit_solution(3652203860662674877)
XLA Ops:
  0.0 2.0 %broadcast_in_dim.8 = bf16[32,128,128]{2,1,0:T(8,128)(2,1)} broadcast(bf16[128,128]{1,0:T(8,128)(2,1)} %tile_ref.1), dimensions={1,2} | broadcast | bytes 1081344 | tf_op jit(solution)/shard_map/broadcast_in_dim | solution.py:77
  2.0 0.0 copy-start
  2.0 10.6 %all-to-all-start = ((bf16[32,128,128]{2,1,0:T(8,128)(2,1)}), bf16[32,128,128]{2,1,0:T(8,128)(2,1)S(1)}, u32[]{:S(2)}, u32[]{:S(2)}) async-start(bf16[32,128,128]{2,1,0:T(8,128)(2,1)} %broadcast_in_dim.8), calls=%async_computation | async-start | bytes 2097152 | tf_op jit(solution)/shard_map/all_to_all | solution.py:79
  12.6 0.0 copy-done
  12.6 43.1 %all-gather = bf16[2048,128]{1,0:T(8,128)(2,1)S(1)} all-gather(bf16[128,128]{1,0:T(8,128)(2,1)S(1)} %copy-done), channel_id=2, replica_groups={{0,96,128,224,256,352,384,480,512,608,640,736,768,864,896,992},{32,64,1..., dimensions={0}, use_global_device_ids=true | all-gather | bytes 557056 | tf_op jit(solution)/shard_map/all_gather | solution.py:67
  55.7 2.3 %collective-permute-start = (bf16[16,128,128]{2,1,0:T(8,128)(2,1)S(1)}, bf16[16,128,128]{2,1,0:T(8,128)(2,1)S(1)}, u32[]{:S(2)}, u32[]{:S(2)}) collective-permute-start(bf16[16,128,128]{2,1,0:T(8,128)(2,1)S(1)} %bitcast.15), channel_id=1, source_target_pairs={{0,32},{32,0},{64,96},{96,64},{128,160},{160,128},{192,224},{224,1... | collective-permute-start | bytes 1572872 | tf_op jit(solution)/shard_map/ppermute | solution.py:69
  58.0 0.0 copy-start.1
  58.0 0.7 copy-done.1
  58.7 0.8 collective-permute-done.other_ref
  59.5 0.0 all-to-all-done.rows_ref
  59.5 1.0 shard_map.28
  60.5 25.8 %all-gather.1 = bf16[2048,128]{1,0:T(8,128)(2,1)S(1)} all-gather(bf16[128,128]{1,0:T(8,128)(2,1)S(1)} %shard_map.28), channel_id=3, replica_groups={{0,96,128,224,256,352,384,480,512,608,640,736,768,864,896,992},{32,64,1..., dimensions={0}, use_global_device_ids=true | all-gather | bytes 557056 | tf_op jit(solution)/shard_map/all_gather | solution.py:67
  86.3 2.2 %collective-permute-start.1 = (bf16[16,128,128]{2,1,0:T(8,128)(2,1)S(1)}, bf16[16,128,128]{2,1,0:T(8,128)(2,1)S(1)}, u32[]{:S(2)}, u32[]{:S(2)}) collective-permute-start(bf16[16,128,128]{2,1,0:T(8,128)(2,1)S(1)} %bitcast.19), channel_id=1, source_target_pairs={{0,32},{32,0},{64,96},{96,64},{128,160},{160,128},{192,224},{224,1... | collective-permute-start | bytes 1572872 | tf_op jit(solution)/shard_map/ppermute | solution.py:69
  88.6 1.5 collective-permute-done.1.other_ref
  90.1 2.1 %shard_map.29 = (bf16[128,128]{1,0:T(8,128)(2,1)S(1)}, bf16[32,128,128]{2,1,0:T(8,128)(2,1)}) custom-call(s32[1]{0:T(128)} %bitcast.ring_ref, s32[2,2]{1,0:T(2,128)S(1)} %get-tuple-element.10.mask_ref, bf16[32,128,128]{2,1,0:T(8,128)(2,1)S(1)} %all-to-all-done.rows_ref, bf16[16,128,128]{2,1,0:T(8,128)(2,1)S(1)} %bitcast.20, ...), custom_call_target="tpu_custom_call" | custom-call | tf_op jit(solution)/shard_map/pallas_call | solution.py:55
  92.2 9.2 %all-to-all-start.1 = ((bf16[32,128,128]{2,1,0:T(8,128)(2,1)}), bf16[32,128,128]{2,1,0:T(8,128)(2,1)S(1)}, u32[]{:S(2)}, u32[]{:S(2)}) async-start(bf16[32,128,128]{2,1,0:T(8,128)(2,1)} %get-tuple-element.7), calls=%async_computation.1 | async-start | bytes 2097152 | tf_op jit(solution)/shard_map/all_to_all | solution.py:79
  101.4 28.6 %all-gather.2 = bf16[2048,128]{1,0:T(8,128)(2,1)S(1)} all-gather(bf16[128,128]{1,0:T(8,128)(2,1)S(1)} %get-tuple-element.8.tile_ref), channel_id=4, replica_groups={{0,96,128,224,256,352,384,480,512,608,640,736,768,864,896,992},{32,64,1..., dimensions={0}, use_global_device_ids=true | all-gather | bytes 557056 | tf_op jit(solution)/shard_map/all_gather | solution.py:67
  130.0 2.1 %collective-permute-start.2 = (bf16[16,128,128]{2,1,0:T(8,128)(2,1)S(1)}, bf16[16,128,128]{2,1,0:T(8,128)(2,1)S(1)}, u32[]{:S(2)}, u32[]{:S(2)}) collective-permute-start(bf16[16,128,128]{2,1,0:T(8,128)(2,1)S(1)} %bitcast.17), channel_id=1, source_target_pairs={{0,32},{32,0},{64,96},{96,64},{128,160},{160,128},{192,224},{224,1... | collective-permute-start | bytes 1572872 | tf_op jit(solution)/shard_map/ppermute | solution.py:69
  132.1 1.7 %collective-permute-done.2.other_ref = bf16[16,128,128]{2,1,0:T(8,128)(2,1)S(1)} collective-permute-done((bf16[16,128,128]{2,1,0:T(8,128)(2,1)S(1)}, bf16[16,128,128]{2,1,0:T(8,128)(2,1)S(1)}, u32[]{:S(2)}, u32[]{:S(2)}) %collective-permute-start.2) | collective-permute-done | bytes 524320 | tf_op jit(solution)/shard_map/ppermute | solution.py:69
  133.8 0.0 all-to-all-done.1.rows_ref
  133.8 1.0 shard_map.30
  134.8 25.4 %all-gather.3 = bf16[2048,128]{1,0:T(8,128)(2,1)S(1)} all-gather(bf16[128,128]{1,0:T(8,128)(2,1)S(1)} %shard_map.30), channel_id=5, replica_groups={{0,96,128,224,256,352,384,480,512,608,640,736,768,864,896,992},{32,64,1..., dimensions={0}, use_global_device_ids=true | all-gather | bytes 557056 | tf_op jit(solution)/shard_map/all_gather | solution.py:67
  160.3 2.2 %collective-permute-start.3 = (bf16[16,128,128]{2,1,0:T(8,128)(2,1)S(1)}, bf16[16,128,128]{2,1,0:T(8,128)(2,1)S(1)}, u32[]{:S(2)}, u32[]{:S(2)}) collective-permute-start(bf16[16,128,128]{2,1,0:T(8,128)(2,1)S(1)} %bitcast.13), channel_id=1, source_target_pairs={{0,32},{32,0},{64,96},{96,64},{128,160},{160,128},{192,224},{224,1... | collective-permute-start | bytes 1572872 | tf_op jit(solution)/shard_map/ppermute | solution.py:69
  162.5 1.5 collective-permute-done.3.other_ref
  164.0 1.6 shard_map.31
  (1 shorter events, 0.0 us)
Async XLA Ops:
  2.0 10.6 %copy-start = (bf16[128,128]{1,0:T(8,128)(2,1)S(1)}, bf16[128,128]{1,0:T(8,128)(2,1)}, u32[]{:S(2)}) copy-start(bf16[128,128]{1,0:T(8,128)(2,1)} %tile_ref.1) | copy-start | bytes 98308
  2.0 57.5 %all-to-all-start = ((bf16[32,128,128]{2,1,0:T(8,128)(2,1)}), bf16[32,128,128]{2,1,0:T(8,128)(2,1)S(1)}, u32[]{:S(2)}, u32[]{:S(2)}) async-start(bf16[32,128,128]{2,1,0:T(8,128)(2,1)} %broadcast_in_dim.8), calls=%async_computation | async-start | bytes 2097152 | tf_op jit(solution)/shard_map/all_to_all | solution.py:79
  55.7 3.8 %collective-permute-start = (bf16[16,128,128]{2,1,0:T(8,128)(2,1)S(1)}, bf16[16,128,128]{2,1,0:T(8,128)(2,1)S(1)}, u32[]{:S(2)}, u32[]{:S(2)}) collective-permute-start(bf16[16,128,128]{2,1,0:T(8,128)(2,1)S(1)} %bitcast.15), channel_id=1, source_target_pairs={{0,32},{32,0},{64,96},{96,64},{128,160},{160,128},{192,224},{224,1... | collective-permute-start | bytes 1572872 | tf_op jit(solution)/shard_map/ppermute | solution.py:69
  58.0 0.7 copy-start.1
  86.3 3.8 %collective-permute-start.1 = (bf16[16,128,128]{2,1,0:T(8,128)(2,1)S(1)}, bf16[16,128,128]{2,1,0:T(8,128)(2,1)S(1)}, u32[]{:S(2)}, u32[]{:S(2)}) collective-permute-start(bf16[16,128,128]{2,1,0:T(8,128)(2,1)S(1)} %bitcast.19), channel_id=1, source_target_pairs={{0,32},{32,0},{64,96},{96,64},{128,160},{160,128},{192,224},{224,1... | collective-permute-start | bytes 1572872 | tf_op jit(solution)/shard_map/ppermute | solution.py:69
  92.2 41.6 %all-to-all-start.1 = ((bf16[32,128,128]{2,1,0:T(8,128)(2,1)}), bf16[32,128,128]{2,1,0:T(8,128)(2,1)S(1)}, u32[]{:S(2)}, u32[]{:S(2)}) async-start(bf16[32,128,128]{2,1,0:T(8,128)(2,1)} %get-tuple-element.7), calls=%async_computation.1 | async-start | bytes 2097152 | tf_op jit(solution)/shard_map/all_to_all | solution.py:79
  130.0 3.8 %collective-permute-start.2 = (bf16[16,128,128]{2,1,0:T(8,128)(2,1)S(1)}, bf16[16,128,128]{2,1,0:T(8,128)(2,1)S(1)}, u32[]{:S(2)}, u32[]{:S(2)}) collective-permute-start(bf16[16,128,128]{2,1,0:T(8,128)(2,1)S(1)} %bitcast.17), channel_id=1, source_target_pairs={{0,32},{32,0},{64,96},{96,64},{128,160},{160,128},{192,224},{224,1... | collective-permute-start | bytes 1572872 | tf_op jit(solution)/shard_map/ppermute | solution.py:69
  160.3 3.8 %collective-permute-start.3 = (bf16[16,128,128]{2,1,0:T(8,128)(2,1)S(1)}, bf16[16,128,128]{2,1,0:T(8,128)(2,1)S(1)}, u32[]{:S(2)}, u32[]{:S(2)}) collective-permute-start(bf16[16,128,128]{2,1,0:T(8,128)(2,1)S(1)} %bitcast.13), channel_id=1, source_target_pairs={{0,32},{32,0},{64,96},{96,64},{128,160},{160,128},{192,224},{224,1... | collective-permute-start | bytes 1572872 | tf_op jit(solution)/shard_map/ppermute | solution.py:69

commit v4 on v3

v4 whole, which is shorter than its diff:
```python
import jax
import jax.numpy as jnp
from jax import lax
from jax.experimental import pallas as pl
from jax.experimental.pallas import tpu as pltpu
from jax.sharding import PartitionSpec as P

BS = 64
ITERS = 2
CORES = 2
PLANE = ("row", "depth")
F32 = jnp.float32
BF16 = jnp.bfloat16


def filtered(value, mask_ref):
    block_row = lax.broadcasted_iota(jnp.int32, value.shape, 0) // BS
    block_col = lax.broadcasted_iota(jnp.int32, value.shape, 1) // BS
    keep = jnp.zeros(value.shape, jnp.int32)
    for i in range(value.shape[0] // BS):
        for j in range(value.shape[1] // BS):
            here = jnp.logical_and(block_row == i, block_col == j)
            keep = jnp.where(here, mask_ref[i, j], keep)
    return jnp.where(keep == 1, value, 0.0).astype(BF16)


def ring_product(ring, rows_ref, col_ref):
    chips, side, cols = col_ref.shape
    cores = [1 - ring if z % 2 else ring for z in range(chips)]
    left = jnp.concatenate([rows_ref[CORES * z + cores[z]] for z in range(chips)], axis=1)
    return jnp.dot(left, col_ref[...].reshape(chips * side, cols), preferred_element_type=F32)


def own_kernel(ring_ref, rows_ref, own_ref, out_ref):
    out_ref[...] = ring_product(ring_ref[0], rows_ref, own_ref)


def square_kernel(ring_ref, mask_ref, rows_ref, own_ref, other_ref, out_ref):
    total = own_ref[...] + ring_product(1 - ring_ref[0], rows_ref, other_ref)
    out_ref[...] = filtered(total, mask_ref)


def update_kernel(ring_ref, mask_ref, rows_ref, own_ref, other_ref, tile_ref, out_ref):
    cube_term = own_ref[...] + ring_product(1 - ring_ref[0], rows_ref, other_ref)
    out_ref[...] = filtered(1.5 * tile_ref[...].astype(F32) - 0.5 * cube_term, mask_ref)


def copy_out(tile_ref, copies_ref, sem):
    made = [pltpu.make_async_copy(tile_ref, copies_ref.at[i], sem.at[i]) for i in range(copies_ref.shape[0])]
    for copy in made:
        copy.start()
    for copy in made:
        copy.wait()


def update_copies_kernel(
    ring_ref, mask_ref, rows_ref, own_ref, other_ref, tile_ref, out_ref, copies_ref, sem
):
    update_kernel(ring_ref, mask_ref, rows_ref, own_ref, other_ref, tile_ref, out_ref)
    copy_out(out_ref, copies_ref, sem)


SMEM = pl.BlockSpec(memory_space=pltpu.SMEM)
VMEM = pl.BlockSpec(memory_space=pltpu.VMEM)
ANY = pl.BlockSpec(memory_space=pl.ANY)


def call(kernel, scalars, arrays, out, copies=0):
    outs, specs, scratch = [out], [VMEM], []
    if copies:
        outs.append(jax.ShapeDtypeStruct((copies, *out.shape), out.dtype))
        specs.append(ANY)
        scratch.append(pltpu.SemaphoreType.DMA((copies,)))
    flops = sum(2 * a.size * out.shape[1] for a in arrays if a.ndim == 3)
    return pl.pallas_call(
        kernel,
        out_shape=outs,
        in_specs=[SMEM] * len(scalars) + [VMEM] * len(arrays),
        out_specs=specs,
        scratch_shapes=scratch,
        cost_estimate=pl.CostEstimate(
            flops=flops, bytes_accessed=sum(2 * a.size for a in arrays), transcendentals=0
        ),
        compiler_params=pltpu.CompilerParams(vmem_limit_bytes=32 << 20),
    )(*scalars, *arrays)


def broadcast(tile, copies):
    return pl.pallas_call(
        copy_out,
        out_shape=jax.ShapeDtypeStruct((copies, *tile.shape), tile.dtype),
        in_specs=[VMEM],
        out_specs=ANY,
        scratch_shapes=[pltpu.SemaphoreType.DMA((copies,))],
    )(tile)


def product(kernel, place, mask, rows, column, more, out, copies=0):
    chips = lax.axis_size("blk") // CORES
    rings = [[CORES * z + (z + p) % CORES for z in range(chips)] for p in range(CORES)]
    swap = [(CORES * z + k, CORES * z + 1 - k) for z in range(chips) for k in range(CORES)]
    ring = ((place // CORES + place) % CORES).astype(jnp.int32).reshape(1)
    own = lax.all_gather(column, "blk", axis=0, axis_index_groups=rings)
    other = lax.ppermute(own, "blk", swap)
    (half,) = call(own_kernel, [ring], [rows, own], jax.ShapeDtypeStruct(out.shape, F32))
    return call(kernel, [ring, mask], [rows, half, other, *more], out, copies)


def on_device(x_start, keep_mask):
    tiles = lax.axis_size(PLANE)
    place = lax.axis_index("blk")
    out = jax.ShapeDtypeStruct(x_start.shape, BF16)
    tile, copies = x_start, broadcast(x_start, tiles)
    for step in range(ITERS):
        rows = lax.all_to_all(copies, PLANE, 0, 0)
        (square,) = product(square_kernel, place, keep_mask[step, 0], rows, tile, [], out)
        if step < ITERS - 1:
            tile, copies = product(
                update_copies_kernel, place, keep_mask[step, 1], rows, square, [tile], out, tiles
            )
        else:
            (tile,) = product(update_kernel, place, keep_mask[step, 1], rows, square, [tile], out)
    return tile


def solution(mesh):
    spec = P("blk", PLANE)
    return jax.shard_map(
        on_device,
        mesh=mesh,
        in_specs=(spec, P(None, None, "blk", PLANE)),
        out_specs=spec,
        check_vma=False,
    )
```

time: 166 us -> 166 us (level)
  Pallas kernels: 5.65 us -> 8.39 us
  local copies, waits for them, and re-layouts: 2.65 us -> 0.68 us
    pallas_call x4 -> x9, Pallas kernels: 5.65 us -> 8.39 us  [the longest x8 6.38 us: call(): pl.pallas_call(kernel, out_shape=outs, in_specs=[SMEM] * len(scalars) + [...]
    broadcast_in_dim x1 -> x0, local copies, waits for them, and re-layouts: 1.96 us -> none  [on_device(): jnp.broadcast_to(x_start[None], (tiles, side, side))]
  transfers between devices with their start and end apart: 6 -> 6, of which waited for: 4 -> 4; matrix products, arithmetic and copies ran while one was open for 0% -> 0% of each run, Pallas kernels for 0% -> 1%
where the time goes in v4:
time: 166 us; the launch traced here: 165 us
  blocking collectives  123 us (74%)
  starting transfers between devices  28.6 us (17%)
  Pallas kernels  8.39 us (5%)
  waiting for transfers between devices  4.4 us (3%)
    all_gather x4, blocking collectives, product(): own = lax.all_gather(column, 'blk', axis=0, axis_index_groups=rings)  123 us
    all_to_all x2, starting transfers between devices, on_device(): rows = lax.all_to_all(copies, PLANE, 0, 0)  19.7 us
    ppermute x4, starting transfers between devices, product(): other = lax.ppermute(own, 'blk', swap)  8.86 us
    pallas_call x8, Pallas kernels, call(): pl.pallas_call(kernel, out_shape=outs, in_specs=[SMEM] * len(scalars) + [...  6.38 us
    ppermute x4, waiting for transfers between devices, product(): other = lax.ppermute(own, 'blk', swap)  4.4 us
  transfers between devices with their start and end apart: 6, of which 4 were waited for; matrix products, arithmetic and copies ran while one was open for 0% of the time, Pallas kernels for 1%

profile of v4, /device:TPU:1, one launch (start us, length us, event | category | flops | bytes accessed | tf_op | source)
XLA Modules:
  0.0 165.2 jit_solution(315088876149744158)
XLA Ops:
  0.0 2.0 %shard_map.28 = bf16[32,128,128]{2,1,0:T(8,128)(2,1)} custom-call(bf16[128,128]{1,0:T(8,128)(2,1)} %tile_ref.3), custom_call_target="tpu_custom_call" | custom-call | tf_op jit(solution)/shard_map/pallas_call | solution.py:89
  2.0 0.0 copy-start
  2.0 10.5 %all-to-all-start = ((bf16[32,128,128]{2,1,0:T(8,128)(2,1)}), bf16[32,128,128]{2,1,0:T(8,128)(2,1)S(1)}, u32[]{:S(2)}, u32[]{:S(2)}) async-start(bf16[32,128,128]{2,1,0:T(8,128)(2,1)} %shard_map.28), calls=%async_computation | async-start | bytes 2097152 | tf_op jit(solution)/shard_map/all_to_all | solution.py:115
  12.6 0.0 copy-done
  12.6 43.1 %all-gather = bf16[2048,128]{1,0:T(8,128)(2,1)S(1)} all-gather(bf16[128,128]{1,0:T(8,128)(2,1)S(1)} %copy-done), channel_id=2, replica_groups={{0,96,128,224,256,352,384,480,512,608,640,736,768,864,896,992},{32,64,1..., dimensions={0}, use_global_device_ids=true | all-gather | bytes 557056 | tf_op jit(solution)/shard_map/all_gather | solution.py:103
  55.6 2.3 %collective-permute-start = (bf16[16,128,128]{2,1,0:T(8,128)(2,1)S(1)}, bf16[16,128,128]{2,1,0:T(8,128)(2,1)S(1)}, u32[]{:S(2)}, u32[]{:S(2)}) collective-permute-start(bf16[16,128,128]{2,1,0:T(8,128)(2,1)S(1)} %bitcast.13), channel_id=1, source_target_pairs={{0,32},{32,0},{64,96},{96,64},{128,160},{160,128},{192,224},{224,1... | collective-permute-start | bytes 1572872 | tf_op jit(solution)/shard_map/ppermute | solution.py:104
  57.9 0.0 copy-start.1
  58.0 0.7 copy-done.1
  58.6 0.0 all-to-all-done.rows_ref
  58.6 0.3 shard_map.29.own_ref
  58.9 0.5 collective-permute-done.other_ref
  59.4 0.8 shard_map.30
  60.3 25.8 %all-gather.1 = bf16[2048,128]{1,0:T(8,128)(2,1)S(1)} all-gather(bf16[128,128]{1,0:T(8,128)(2,1)S(1)} %shard_map.30), channel_id=3, replica_groups={{0,96,128,224,256,352,384,480,512,608,640,736,768,864,896,992},{32,64,1..., dimensions={0}, use_global_device_ids=true | all-gather | bytes 557056 | tf_op jit(solution)/shard_map/all_gather | solution.py:103
  86.1 2.2 %collective-permute-start.1 = (bf16[16,128,128]{2,1,0:T(8,128)(2,1)S(1)}, bf16[16,128,128]{2,1,0:T(8,128)(2,1)S(1)}, u32[]{:S(2)}, u32[]{:S(2)}) collective-permute-start(bf16[16,128,128]{2,1,0:T(8,128)(2,1)S(1)} %bitcast.17), channel_id=1, source_target_pairs={{0,32},{32,0},{64,96},{96,64},{128,160},{160,128},{192,224},{224,1... | collective-permute-start | bytes 1572872 | tf_op jit(solution)/shard_map/ppermute | solution.py:104
  88.4 0.3 shard_map.31.own_ref
  88.7 1.3 collective-permute-done.1.other_ref
  89.9 2.1 %shard_map.32 = (bf16[128,128]{1,0:T(8,128)(2,1)S(1)}, bf16[32,128,128]{2,1,0:T(8,128)(2,1)}) custom-call(s32[1]{0:T(128)} %bitcast.ring_ref, s32[2,2]{1,0:T(2,128)S(1)} %get-tuple-element.10.mask_ref, bf16[32,128,128]{2,1,0:T(8,128)(2,1)S(1)} %all-to-all-done.rows_ref, f32[128,128]{1,0:T(8,128)S(1)} %shard_map.31.own_ref, ...), custom_call_target="tpu_custom_call" | custom-call | flops 201326592 | bytes 1638400 | tf_op jit(solution)/shard_map/pallas_call | solution.py:75
  92.0 9.2 %all-to-all-start.1 = ((bf16[32,128,128]{2,1,0:T(8,128)(2,1)}), bf16[32,128,128]{2,1,0:T(8,128)(2,1)S(1)}, u32[]{:S(2)}, u32[]{:S(2)}) async-start(bf16[32,128,128]{2,1,0:T(8,128)(2,1)} %get-tuple-element.7), calls=%async_computation.1 | async-start | bytes 2097152 | tf_op jit(solution)/shard_map/all_to_all | solution.py:115
  101.3 28.6 %all-gather.2 = bf16[2048,128]{1,0:T(8,128)(2,1)S(1)} all-gather(bf16[128,128]{1,0:T(8,128)(2,1)S(1)} %get-tuple-element.8.tile_ref), channel_id=4, replica_groups={{0,96,128,224,256,352,384,480,512,608,640,736,768,864,896,992},{32,64,1..., dimensions={0}, use_global_device_ids=true | all-gather | bytes 557056 | tf_op jit(solution)/shard_map/all_gather | solution.py:103
  129.9 2.1 %collective-permute-start.2 = (bf16[16,128,128]{2,1,0:T(8,128)(2,1)S(1)}, bf16[16,128,128]{2,1,0:T(8,128)(2,1)S(1)}, u32[]{:S(2)}, u32[]{:S(2)}) collective-permute-start(bf16[16,128,128]{2,1,0:T(8,128)(2,1)S(1)} %bitcast.15), channel_id=1, source_target_pairs={{0,32},{32,0},{64,96},{96,64},{128,160},{160,128},{192,224},{224,1... | collective-permute-start | bytes 1572872 | tf_op jit(solution)/shard_map/ppermute | solution.py:104
  132.0 0.0 all-to-all-done.1.rows_ref
  132.0 0.3 shard_map.33.own_ref
  132.3 1.4 collective-permute-done.2.other_ref
  133.7 0.8 shard_map.34
  134.5 25.4 %all-gather.3 = bf16[2048,128]{1,0:T(8,128)(2,1)S(1)} all-gather(bf16[128,128]{1,0:T(8,128)(2,1)S(1)} %shard_map.34), channel_id=5, replica_groups={{0,96,128,224,256,352,384,480,512,608,640,736,768,864,896,992},{32,64,1..., dimensions={0}, use_global_device_ids=true | all-gather | bytes 557056 | tf_op jit(solution)/shard_map/all_gather | solution.py:103
  160.0 2.2 %collective-permute-start.3 = (bf16[16,128,128]{2,1,0:T(8,128)(2,1)S(1)}, bf16[16,128,128]{2,1,0:T(8,128)(2,1)S(1)}, u32[]{:S(2)}, u32[]{:S(2)}) collective-permute-start(bf16[16,128,128]{2,1,0:T(8,128)(2,1)S(1)} %bitcast.19), channel_id=1, source_target_pairs={{0,32},{32,0},{64,96},{96,64},{128,160},{160,128},{192,224},{224,1... | collective-permute-start | bytes 1572872 | tf_op jit(solution)/shard_map/ppermute | solution.py:104
  162.2 0.3 shard_map.35.own_ref
  162.5 1.3 collective-permute-done.3.other_ref
  163.8 1.5 shard_map.36
  (1 shorter events, 0.0 us)
Async XLA Ops:
  2.0 10.5 %copy-start = (bf16[128,128]{1,0:T(8,128)(2,1)S(1)}, bf16[128,128]{1,0:T(8,128)(2,1)}, u32[]{:S(2)}) copy-start(bf16[128,128]{1,0:T(8,128)(2,1)} %tile_ref.3) | copy-start | bytes 98308
  2.0 56.6 %all-to-all-start = ((bf16[32,128,128]{2,1,0:T(8,128)(2,1)}), bf16[32,128,128]{2,1,0:T(8,128)(2,1)S(1)}, u32[]{:S(2)}, u32[]{:S(2)}) async-start(bf16[32,128,128]{2,1,0:T(8,128)(2,1)} %shard_map.28), calls=%async_computation | async-start | bytes 2097152 | tf_op jit(solution)/shard_map/all_to_all | solution.py:115
  55.6 3.8 %collective-permute-start = (bf16[16,128,128]{2,1,0:T(8,128)(2,1)S(1)}, bf16[16,128,128]{2,1,0:T(8,128)(2,1)S(1)}, u32[]{:S(2)}, u32[]{:S(2)}) collective-permute-start(bf16[16,128,128]{2,1,0:T(8,128)(2,1)S(1)} %bitcast.13), channel_id=1, source_target_pairs={{0,32},{32,0},{64,96},{96,64},{128,160},{160,128},{192,224},{224,1... | collective-permute-start | bytes 1572872 | tf_op jit(solution)/shard_map/ppermute | solution.py:104
  57.9 0.7 copy-start.1
  86.1 3.8 %collective-permute-start.1 = (bf16[16,128,128]{2,1,0:T(8,128)(2,1)S(1)}, bf16[16,128,128]{2,1,0:T(8,128)(2,1)S(1)}, u32[]{:S(2)}, u32[]{:S(2)}) collective-permute-start(bf16[16,128,128]{2,1,0:T(8,128)(2,1)S(1)} %bitcast.17), channel_id=1, source_target_pairs={{0,32},{32,0},{64,96},{96,64},{128,160},{160,128},{192,224},{224,1... | collective-permute-start | bytes 1572872 | tf_op jit(solution)/shard_map/ppermute | solution.py:104
  92.0 40.0 %all-to-all-start.1 = ((bf16[32,128,128]{2,1,0:T(8,128)(2,1)}), bf16[32,128,128]{2,1,0:T(8,128)(2,1)S(1)}, u32[]{:S(2)}, u32[]{:S(2)}) async-start(bf16[32,128,128]{2,1,0:T(8,128)(2,1)} %get-tuple-element.7), calls=%async_computation.1 | async-start | bytes 2097152 | tf_op jit(solution)/shard_map/all_to_all | solution.py:115
  129.9 3.8 %collective-permute-start.2 = (bf16[16,128,128]{2,1,0:T(8,128)(2,1)S(1)}, bf16[16,128,128]{2,1,0:T(8,128)(2,1)S(1)}, u32[]{:S(2)}, u32[]{:S(2)}) collective-permute-start(bf16[16,128,128]{2,1,0:T(8,128)(2,1)S(1)} %bitcast.15), channel_id=1, source_target_pairs={{0,32},{32,0},{64,96},{96,64},{128,160},{160,128},{192,224},{224,1... | collective-permute-start | bytes 1572872 | tf_op jit(solution)/shard_map/ppermute | solution.py:104
  160.0 3.8 %collective-permute-start.3 = (bf16[16,128,128]{2,1,0:T(8,128)(2,1)S(1)}, bf16[16,128,128]{2,1,0:T(8,128)(2,1)S(1)}, u32[]{:S(2)}, u32[]{:S(2)}) collective-permute-start(bf16[16,128,128]{2,1,0:T(8,128)(2,1)S(1)} %bitcast.19), channel_id=1, source_target_pairs={{0,32},{32,0},{64,96},{96,64},{128,160},{160,128},{192,224},{224,1... | collective-permute-start | bytes 1572872 | tf_op jit(solution)/shard_map/ppermute | solution.py:104

commit v5 on v4

v5 whole, which is shorter than its diff:
```python
import functools

import jax
import jax.numpy as jnp
from jax import lax
from jax.experimental import pallas as pl
from jax.experimental.pallas import tpu as pltpu
from jax.sharding import PartitionSpec as P

BS = 64
ITERS = 2
CORES = 2
PLANE = ("row", "depth")
F32 = jnp.float32
BF16 = jnp.bfloat16


def ring_rows(ring, rows_ref):
    chips = rows_ref.shape[0] // CORES
    cores = [1 - ring if z % 2 else ring for z in range(chips)]
    return jnp.concatenate([rows_ref[CORES * z + cores[z]] for z in range(chips)], axis=1)


def times(left, column_ref):
    chips, side, cols = column_ref.shape
    return jnp.dot(left, column_ref[...].reshape(chips * side, cols), preferred_element_type=F32)


def expanded(mask_ref, shape):
    block_row = lax.broadcasted_iota(jnp.int32, shape, 0) // BS
    block_col = lax.broadcasted_iota(jnp.int32, shape, 1) // BS
    keep = jnp.zeros(shape, jnp.int32)
    for i in range(shape[0] // BS):
        for j in range(shape[1] // BS):
            here = jnp.logical_and(block_row == i, block_col == j)
            keep = jnp.where(here, mask_ref[i, j], keep)
    return keep


def own_kernel(scale, ring_ref, mask_ref, rows_ref, own_ref, *refs):
    *tile_ref, base_ref, left_ref, keep_ref = refs
    ring = ring_ref[0]
    base = scale * times(ring_rows(ring, rows_ref), own_ref)
    if tile_ref:
        base = 1.5 * tile_ref[0][...].astype(F32) + base
    base_ref[...] = base
    left_ref[...] = ring_rows(1 - ring, rows_ref)
    keep_ref[...] = expanded(mask_ref, keep_ref.shape)


def other_kernel(scale, base_ref, left_ref, keep_ref, other_ref, out_ref):
    total = base_ref[...] + scale * times(left_ref[...], other_ref)
    out_ref[...] = jnp.where(keep_ref[...] == 1, total, 0.0).astype(BF16)


def copy_out(tile, copies_ref, few_ref, sem):
    few = few_ref.shape[0]
    for i in range(few):
        few_ref[i] = tile
    made = [
        pltpu.make_async_copy(few_ref, copies_ref.at[pl.ds(few * i, few)], sem.at[i])
        for i in range(copies_ref.shape[0] // few)
    ]
    for copy in made:
        copy.start()
    for copy in made:
        copy.wait()


def other_copies_kernel(
    scale, base_ref, left_ref, keep_ref, other_ref, out_ref, copies_ref, few_ref, sem
):
    other_kernel(scale, base_ref, left_ref, keep_ref, other_ref, out_ref)
    copy_out(out_ref[...], copies_ref, few_ref, sem)


def broadcast_kernel(tile_ref, copies_ref, few_ref, sem):
    copy_out(tile_ref[...], copies_ref, few_ref, sem)


FEW = 4
SMEM = pl.BlockSpec(memory_space=pltpu.SMEM)
VMEM = pl.BlockSpec(memory_space=pltpu.VMEM)
ANY = pl.BlockSpec(memory_space=pl.ANY)


def call(kernel, scalars, arrays, outs, copies=0):
    specs, scratch = [VMEM] * len(outs), []
    if copies:
        shape = arrays[0].shape if not outs else outs[0].shape
        outs = [*outs, jax.ShapeDtypeStruct((copies, *shape), BF16)]
        specs.append(ANY)
        scratch = [pltpu.VMEM((FEW, *shape), BF16), pltpu.SemaphoreType.DMA((copies // FEW,))]
    work = sum(a.size for a in arrays)
    return pl.pallas_call(
        kernel,
        out_shape=outs,
        in_specs=[SMEM] * len(scalars) + [VMEM] * len(arrays),
        out_specs=specs,
        scratch_shapes=scratch,
        cost_estimate=pl.CostEstimate(
            flops=256 * work, bytes_accessed=2 * work, transcendentals=0
        ),
        compiler_params=pltpu.CompilerParams(vmem_limit_bytes=32 << 20),
    )(*scalars, *arrays)


def product(place, mask, rows, column, tile=None, copies=0):
    side, cols = column.shape
    chips = lax.axis_size("blk") // CORES
    rings = [[CORES * z + (z + p) % CORES for z in range(chips)] for p in range(CORES)]
    swap = [(CORES * z + k, CORES * z + 1 - k) for z in range(chips) for k in range(CORES)]
    ring = ((place // CORES + place) % CORES).astype(jnp.int32).reshape(1)
    own = lax.all_gather(column, "blk", axis=0, axis_index_groups=rings)
    other = lax.ppermute(own, "blk", swap)
    scale = 1.0 if tile is None else -0.5
    parts = call(
        functools.partial(own_kernel, scale),
        [ring, mask],
        [rows, own] + ([] if tile is None else [tile]),
        [
            jax.ShapeDtypeStruct((side, cols), F32),
            jax.ShapeDtypeStruct((side, chips * side), BF16),
            jax.ShapeDtypeStruct((side, cols), jnp.int32),
        ],
    )
    last = functools.partial(other_copies_kernel if copies else other_kernel, scale)
    return call(last, [], [*parts, other], [jax.ShapeDtypeStruct((side, cols), BF16)], copies)


def on_device(x_start, keep_mask):
    tiles = lax.axis_size(PLANE)
    place = lax.axis_index("blk")
    tile, (copies,) = x_start, call(broadcast_kernel, [], [x_start], [], tiles)
    for step in range(ITERS):
        rows = lax.all_to_all(copies, PLANE, 0, 0)
        (square,) = product(place, keep_mask[step, 0], rows, tile)
        more = tiles if step < ITERS - 1 else 0
        tile, *copies = product(place, keep_mask[step, 1], rows, square, tile, more)
        copies = copies[0] if copies else None
    return tile


def solution(mesh):
    spec = P("blk", PLANE)
    return jax.shard_map(
        on_device,
        mesh=mesh,
        in_specs=(spec, P(None, None, "blk", PLANE)),
        out_specs=spec,
        check_vma=False,
    )
```

time: 166 us -> 163 us (0.982)
  waiting for transfers between devices: 4.4 us -> 2.36 us
    ppermute x4, waiting for transfers between devices: 4.4 us -> 2.35 us  [product(): other = lax.ppermute(own, 'blk', swap)]
    pallas_call x1 -> x0, Pallas kernels: 2.01 us -> none  [broadcast(): pl.pallas_call(copy_out, out_shape=jax.ShapeDtypeStruct((copies, *tile.sh...]
    pallas_call x8 -> x9, Pallas kernels: 6.38 us -> 7.34 us  [call(): pl.pallas_call(kernel, out_shape=outs, in_specs=[SMEM] * len(scalars) + [...]
  transfers between devices with their start and end apart: 6 -> 6, of which waited for: 4 -> 3; matrix products, arithmetic and copies ran while one was open for 0% -> 0% of each run, Pallas kernels for 1% -> 2%
where the time goes in v5:
time: 163 us
  blocking collectives  123 us (75%)
  starting transfers between devices  28.4 us (17%)
  Pallas kernels  7.34 us (5%)
  waiting for transfers between devices  2.36 us (1%)
    all_gather x4, blocking collectives, product(): own = lax.all_gather(column, 'blk', axis=0, axis_index_groups=rings)  123 us
    all_to_all x2, starting transfers between devices, on_device(): rows = lax.all_to_all(copies, PLANE, 0, 0)  19.8 us
    ppermute x4, starting transfers between devices, product(): other = lax.ppermute(own, 'blk', swap)  8.67 us
    pallas_call x9, Pallas kernels, call(): pl.pallas_call(kernel, out_shape=outs, in_specs=[SMEM] * len(scalars) + [...  7.34 us
  transfers between devices with their start and end apart: 6, of which 3 were waited for; matrix products, arithmetic and copies ran while one was open for 0% of the time, Pallas kernels for 2%

profile of v5, /device:TPU:1, one launch (start us, length us, event | category | flops | bytes accessed | tf_op | source)
XLA Modules:
  0.0 162.6 jit_solution(15329060558032261322)
XLA Ops:
  0.0 0.0 copy-start
  0.0 0.8 copy-done
  0.8 1.1 shard_map.28
  1.8 0.0 copy-start.1
  1.8 10.5 %all-to-all-start = ((bf16[32,128,128]{2,1,0:T(8,128)(2,1)}), bf16[32,128,128]{2,1,0:T(8,128)(2,1)S(1)}, u32[]{:S(2)}, u32[]{:S(2)}) async-start(bf16[32,128,128]{2,1,0:T(8,128)(2,1)} %shard_map.28), calls=%async_computation | async-start | bytes 2097152 | tf_op jit(solution)/shard_map/all_to_all | solution.py:136
  12.4 0.0 copy-done.1
  12.4 43.1 %all-gather = bf16[2048,128]{1,0:T(8,128)(2,1)S(1)} all-gather(bf16[128,128]{1,0:T(8,128)(2,1)S(1)} %copy-done.1), channel_id=2, replica_groups={{0,96,128,224,256,352,384,480,512,608,640,736,768,864,896,992},{32,64,1..., dimensions={0}, use_global_device_ids=true | all-gather | bytes 557056 | tf_op jit(solution)/shard_map/all_gather | solution.py:114
  55.4 2.3 %collective-permute-start = (bf16[16,128,128]{2,1,0:T(8,128)(2,1)S(1)}, bf16[16,128,128]{2,1,0:T(8,128)(2,1)S(1)}, u32[]{:S(2)}, u32[]{:S(2)}) collective-permute-start(bf16[16,128,128]{2,1,0:T(8,128)(2,1)S(1)} %bitcast.13), channel_id=1, source_target_pairs={{0,32},{32,0},{64,96},{96,64},{128,160},{160,128},{192,224},{224,1... | collective-permute-start | bytes 1572872 | tf_op jit(solution)/shard_map/ppermute | solution.py:115
  57.7 0.0 copy-start.2
  57.8 0.7 copy-done.2
  58.4 0.0 all-to-all-done.rows_ref
  58.4 0.9 shard_map.29
  59.3 0.0 collective-permute-done.other_ref
  59.3 0.3 shard_map.30
  59.6 25.8 %all-gather.1 = bf16[2048,128]{1,0:T(8,128)(2,1)S(1)} all-gather(bf16[128,128]{1,0:T(8,128)(2,1)S(1)} %shard_map.30), channel_id=3, replica_groups={{0,96,128,224,256,352,384,480,512,608,640,736,768,864,896,992},{32,64,1..., dimensions={0}, use_global_device_ids=true | all-gather | bytes 557056 | tf_op jit(solution)/shard_map/all_gather | solution.py:114
  85.4 2.2 %collective-permute-start.1 = (bf16[16,128,128]{2,1,0:T(8,128)(2,1)S(1)}, bf16[16,128,128]{2,1,0:T(8,128)(2,1)S(1)}, u32[]{:S(2)}, u32[]{:S(2)}) collective-permute-start(bf16[16,128,128]{2,1,0:T(8,128)(2,1)S(1)} %bitcast.19), channel_id=1, source_target_pairs={{0,32},{32,0},{64,96},{96,64},{128,160},{160,128},{192,224},{224,1... | collective-permute-start | bytes 1572872 | tf_op jit(solution)/shard_map/ppermute | solution.py:115
  87.6 0.9 shard_map.31
  88.5 0.7 collective-permute-done.1.other_ref
  89.2 1.4 shard_map.32
  90.5 9.2 %all-to-all-start.1 = ((bf16[32,128,128]{2,1,0:T(8,128)(2,1)}), bf16[32,128,128]{2,1,0:T(8,128)(2,1)S(1)}, u32[]{:S(2)}, u32[]{:S(2)}) async-start(bf16[32,128,128]{2,1,0:T(8,128)(2,1)} %get-tuple-element.25), calls=%async_computation.1 | async-start | bytes 2097152 | tf_op jit(solution)/shard_map/all_to_all | solution.py:136
  99.8 28.6 %all-gather.2 = bf16[2048,128]{1,0:T(8,128)(2,1)S(1)} all-gather(bf16[128,128]{1,0:T(8,128)(2,1)S(1)} %get-tuple-element.26.refs_0_), channel_id=4, replica_groups={{0,96,128,224,256,352,384,480,512,608,640,736,768,864,896,992},{32,64,1..., dimensions={0}, use_global_device_ids=true | all-gather | bytes 557056 | tf_op jit(solution)/shard_map/all_gather | solution.py:114
  128.4 1.9 %collective-permute-start.2 = (bf16[16,128,128]{2,1,0:T(8,128)(2,1)S(1)}, bf16[16,128,128]{2,1,0:T(8,128)(2,1)S(1)}, u32[]{:S(2)}, u32[]{:S(2)}) collective-permute-start(bf16[16,128,128]{2,1,0:T(8,128)(2,1)S(1)} %bitcast.15), channel_id=1, source_target_pairs={{0,32},{32,0},{64,96},{96,64},{128,160},{160,128},{192,224},{224,1... | collective-permute-start | bytes 1572872 | tf_op jit(solution)/shard_map/ppermute | solution.py:115
  130.4 0.0 all-to-all-done.1.rows_ref
  130.4 0.9 shard_map.33
  131.2 1.0 collective-permute-done.2.other_ref
  132.2 0.3 shard_map.34
  132.5 25.4 %all-gather.3 = bf16[2048,128]{1,0:T(8,128)(2,1)S(1)} all-gather(bf16[128,128]{1,0:T(8,128)(2,1)S(1)} %shard_map.34), channel_id=5, replica_groups={{0,96,128,224,256,352,384,480,512,608,640,736,768,864,896,992},{32,64,1..., dimensions={0}, use_global_device_ids=true | all-gather | bytes 557056 | tf_op jit(solution)/shard_map/all_gather | solution.py:114
  157.9 2.2 %collective-permute-start.3 = (bf16[16,128,128]{2,1,0:T(8,128)(2,1)S(1)}, bf16[16,128,128]{2,1,0:T(8,128)(2,1)S(1)}, u32[]{:S(2)}, u32[]{:S(2)}) collective-permute-start(bf16[16,128,128]{2,1,0:T(8,128)(2,1)S(1)} %bitcast.17), channel_id=1, source_target_pairs={{0,32},{32,0},{64,96},{96,64},{128,160},{160,128},{192,224},{224,1... | collective-permute-start | bytes 1572872 | tf_op jit(solution)/shard_map/ppermute | solution.py:115
  160.2 0.9 shard_map.35
  161.0 0.7 collective-permute-done.3.other_ref
  161.7 0.9 shard_map.36
  (1 shorter events, 0.0 us)
Async XLA Ops:
  0.0 0.8 copy-start
  1.8 10.5 %copy-start.1 = (bf16[128,128]{1,0:T(8,128)(2,1)S(1)}, bf16[128,128]{1,0:T(8,128)(2,1)}, u32[]{:S(2)}) copy-start(bf16[128,128]{1,0:T(8,128)(2,1)} %refs_0_.1) | copy-start | bytes 98308
  1.8 56.6 %all-to-all-start = ((bf16[32,128,128]{2,1,0:T(8,128)(2,1)}), bf16[32,128,128]{2,1,0:T(8,128)(2,1)S(1)}, u32[]{:S(2)}, u32[]{:S(2)}) async-start(bf16[32,128,128]{2,1,0:T(8,128)(2,1)} %shard_map.28), calls=%async_computation | async-start | bytes 2097152 | tf_op jit(solution)/shard_map/all_to_all | solution.py:136
  55.4 3.9 %collective-permute-start = (bf16[16,128,128]{2,1,0:T(8,128)(2,1)S(1)}, bf16[16,128,128]{2,1,0:T(8,128)(2,1)S(1)}, u32[]{:S(2)}, u32[]{:S(2)}) collective-permute-start(bf16[16,128,128]{2,1,0:T(8,128)(2,1)S(1)} %bitcast.13), channel_id=1, source_target_pairs={{0,32},{32,0},{64,96},{96,64},{128,160},{160,128},{192,224},{224,1... | collective-permute-start | bytes 1572872 | tf_op jit(solution)/shard_map/ppermute | solution.py:115
  57.7 0.7 copy-start.2
  85.4 3.8 %collective-permute-start.1 = (bf16[16,128,128]{2,1,0:T(8,128)(2,1)S(1)}, bf16[16,128,128]{2,1,0:T(8,128)(2,1)S(1)}, u32[]{:S(2)}, u32[]{:S(2)}) collective-permute-start(bf16[16,128,128]{2,1,0:T(8,128)(2,1)S(1)} %bitcast.19), channel_id=1, source_target_pairs={{0,32},{32,0},{64,96},{96,64},{128,160},{160,128},{192,224},{224,1... | collective-permute-start | bytes 1572872 | tf_op jit(solution)/shard_map/ppermute | solution.py:115
  90.5 39.8 %all-to-all-start.1 = ((bf16[32,128,128]{2,1,0:T(8,128)(2,1)}), bf16[32,128,128]{2,1,0:T(8,128)(2,1)S(1)}, u32[]{:S(2)}, u32[]{:S(2)}) async-start(bf16[32,128,128]{2,1,0:T(8,128)(2,1)} %get-tuple-element.25), calls=%async_computation.1 | async-start | bytes 2097152 | tf_op jit(solution)/shard_map/all_to_all | solution.py:136
  128.4 3.8 %collective-permute-start.2 = (bf16[16,128,128]{2,1,0:T(8,128)(2,1)S(1)}, bf16[16,128,128]{2,1,0:T(8,128)(2,1)S(1)}, u32[]{:S(2)}, u32[]{:S(2)}) collective-permute-start(bf16[16,128,128]{2,1,0:T(8,128)(2,1)S(1)} %bitcast.15), channel_id=1, source_target_pairs={{0,32},{32,0},{64,96},{96,64},{128,160},{160,128},{192,224},{224,1... | collective-permute-start | bytes 1572872 | tf_op jit(solution)/shard_map/ppermute | solution.py:115
  157.9 3.8 %collective-permute-start.3 = (bf16[16,128,128]{2,1,0:T(8,128)(2,1)S(1)}, bf16[16,128,128]{2,1,0:T(8,128)(2,1)S(1)}, u32[]{:S(2)}, u32[]{:S(2)}) collective-permute-start(bf16[16,128,128]{2,1,0:T(8,128)(2,1)S(1)} %bitcast.17), channel_id=1, source_target_pairs={{0,32},{32,0},{64,96},{96,64},{128,160},{160,128},{192,224},{224,1... | collective-permute-start | bytes 1572872 | tf_op jit(solution)/shard_map/ppermute | solution.py:115

commit v6 on v0

v6 whole, which is shorter than its diff:
```python
import functools

import jax
import jax.numpy as jnp
from jax import lax
from jax.experimental import pallas as pl
from jax.experimental.pallas import tpu as pltpu
from jax.sharding import PartitionSpec as P

BS = 64
ITERS = 2
CORES = 2
PLANE = ("row", "depth")
FEW = 4
F32 = jnp.float32
BF16 = jnp.bfloat16


def lanes(shape):
    return lax.broadcasted_iota(jnp.int32, shape, len(shape) - 1)


def pieces(values, place_ref):
    side = values[0].shape[0]
    half = side // 2
    ring, odd = place_ref[0:1, :] == 1, place_ref[1:2, :] == 1
    first = jnp.where(odd, values[1], values[0])
    second = jnp.where(odd, values[0], values[1])
    left = jnp.where(ring, pltpu.roll(first, half, 1), first)
    right = jnp.where(ring, second, pltpu.roll(second, half, 1))
    row_piece = jnp.where(lanes((side, side)) < half, left, right)
    column_piece = jnp.concatenate(
        [jnp.where(ring, value[half:], value[:half]) for value in values], axis=0
    )
    return row_piece.astype(BF16), column_piece.astype(BF16)


def copy_out(tile, copies_ref, few_ref, sem):
    few = few_ref.shape[0]
    for i in range(few):
        few_ref[i] = tile
    made = [
        pltpu.make_async_copy(few_ref, copies_ref.at[pl.ds(few * i, few)], sem.at[i])
        for i in range(copies_ref.shape[0] // few)
    ]
    for copy in made:
        copy.start()
    for copy in made:
        copy.wait()


def place_kernel(mask_ref, place_ref, entry_ref):
    width = entry_ref.shape[1]
    blk = lax.axis_index("blk")
    ring = (blk // CORES + blk) % CORES
    for i, value in enumerate((ring, lax.axis_index(PLANE) % CORES, blk % CORES)):
        place_ref[i : i + 1, :] = jnp.full((1, width), value, jnp.int32)
    row = 0
    for step in range(mask_ref.shape[0]):
        for which in range(mask_ref.shape[1]):
            for i in range(mask_ref.shape[2]):
                for j in range(mask_ref.shape[3]):
                    value = mask_ref[step, which, i, j].astype(F32)
                    entry_ref[row : row + 1, :] = jnp.full((1, width), value, F32)
                    row += 1


def first_kernel(both_ref, place_ref, column_ref, copies_ref, few_ref, sem):
    values = [both_ref[i].astype(F32) for i in range(CORES)]
    row_piece, column_piece = pieces(values, place_ref)
    column_ref[...] = column_piece
    copy_out(row_piece, copies_ref, few_ref, sem)


def partial_sums(rows_ref, columns_ref):
    chips, side, cols = columns_ref.shape
    half = side // 2
    low = lanes((side, side)) < half
    even = [rows_ref[CORES * z] for z in range(chips)]
    odd = [rows_ref[CORES * z + 1] for z in range(chips)]
    left0 = jnp.concatenate([jnp.where(low, e, o) for e, o in zip(even, odd)], axis=1)
    left1 = jnp.concatenate([jnp.where(low, o, e) for e, o in zip(even, odd)], axis=1)
    right0 = columns_ref[...].reshape(chips * side, cols)
    right1 = jnp.concatenate(
        [columns_ref[z, h * half : (h + 1) * half] for z in range(chips) for h in (1, 0)], axis=0
    )
    return [
        jnp.dot(left, right, preferred_element_type=F32)
        for left, right in ((left0, right0), (left1, right1))
    ]


def partial_kernel(rows_ref, columns_ref, *refs):
    *entry_ref, out_ref = refs
    side = columns_ref.shape[1]
    for i, value in enumerate(partial_sums(rows_ref, columns_ref)):
        out_ref[i * side : (i + 1) * side, :] = value
    if entry_ref:
        out_ref[CORES * side :, :] = entry_ref[0][...]


def filtered(value, entries, number):
    side = value.shape[0]
    each = side // BS
    low = lanes((1, value.shape[1])) < BS
    rows = []
    for i in range(each):
        at = (number * each + i) * each
        rows.append(jnp.where(low, entries[at : at + 1, :], entries[at + 1 : at + 2, :]))
    block_row = lax.broadcasted_iota(jnp.int32, value.shape, 0) // BS
    keep = jnp.where(block_row == 0, rows[0], rows[1])
    return jnp.where(keep == 1.0, value, 0.0).astype(BF16).astype(F32)


def square_kernel(first, number, sums_ref, *refs):
    if first:
        place_ref, column_ref, entries_ref = refs
        side = column_ref.shape[0]
        for i in range(CORES):
            entries_ref[i] = sums_ref[i, CORES * side :, :]
    else:
        place_ref, entries_ref, column_ref = refs
        side = column_ref.shape[0]
    values = []
    for i in range(CORES):
        at = slice(i * side, (i + 1) * side)
        values.append(filtered(sums_ref[0, at, :] + sums_ref[1, at, :], entries_ref[i], number))
    column_ref[...] = pieces(values, place_ref)[1]


def updated(number, sums_ref, entries_ref, both_ref):
    side = both_ref.shape[1]
    values = []
    for i in range(CORES):
        at = slice(i * side, (i + 1) * side)
        cube_term = sums_ref[0, at, :] + sums_ref[1, at, :]
        value = 1.5 * both_ref[i].astype(F32) - 0.5 * cube_term
        values.append(filtered(value, entries_ref[i], number))
    return values


def update_kernel(
    number, sums_ref, place_ref, entries_ref, both_ref, new_ref, column_ref, copies_ref, few_ref, sem
):
    values = updated(number, sums_ref, entries_ref, both_ref)
    for i in range(CORES):
        new_ref[i] = values[i].astype(BF16)
    row_piece, column_piece = pieces(values, place_ref)
    column_ref[...] = column_piece
    copy_out(row_piece, copies_ref, few_ref, sem)


def last_kernel(number, sums_ref, place_ref, entries_ref, both_ref, out_ref):
    values = updated(number, sums_ref, entries_ref, both_ref)
    out_ref[...] = jnp.where(place_ref[2:3, :] == 1, values[1], values[0]).astype(BF16)


def call(kernel, scalars, arrays, outs, copies=None):
    specs, scratch = [pl.BlockSpec(memory_space=pltpu.VMEM)] * len(outs), []
    if copies is not None:
        outs = [*outs, copies]
        specs.append(pl.BlockSpec(memory_space=pl.ANY))
        few, number = (FEW, *copies.shape[1:]), copies.shape[0] // FEW
        scratch = [pltpu.VMEM(few, copies.dtype), pltpu.SemaphoreType.DMA((number,))]
    work = sum(a.size for a in arrays)
    return pl.pallas_call(
        kernel,
        out_shape=outs,
        in_specs=[pl.BlockSpec(memory_space=pltpu.SMEM)] * len(scalars)
        + [pl.BlockSpec(memory_space=pltpu.VMEM)] * len(arrays),
        out_specs=specs,
        scratch_shapes=scratch,
        cost_estimate=pl.CostEstimate(
            flops=256 * work, bytes_accessed=2 * work, transcendentals=0
        ),
        compiler_params=pltpu.CompilerParams(vmem_limit_bytes=32 << 20),
    )(*scalars, *arrays)


def on_device(x_start, keep_mask):
    side, cols = x_start.shape
    tiles = lax.axis_size(PLANE)
    chips = lax.axis_size("blk") // CORES
    rings = [[CORES * z + (z + p) % CORES for z in range(chips)] for p in range(CORES)]
    pairs = [[CORES * z + k for k in range(CORES)] for z in range(chips)]

    shape = jax.ShapeDtypeStruct
    tile = shape((side, cols), BF16)
    two_tiles = shape((CORES, side, cols), BF16)
    copied = shape((tiles, side, cols), BF16)
    entry = shape((keep_mask.size, cols), F32)

    def between_cores(value):
        return lax.all_gather(value, "blk", axis=0, axis_index_groups=pairs)

    def summed(rows, column, more=()):
        columns = lax.all_gather(column, "blk", axis=0, axis_index_groups=rings)
        height = CORES * side + sum(a.shape[0] for a in more)
        (partial,) = call(partial_kernel, [], [rows, columns, *more], [shape((height, cols), F32)])
        return between_cores(partial)

    place, entries = call(place_kernel, [keep_mask], [], [shape((8, cols), jnp.int32), entry])
    place, entries, x_start = lax.optimization_barrier((place, entries, x_start))
    both = between_cores(x_start)
    column, copies = call(first_kernel, [], [both, place], [tile], copied)
    for step in range(ITERS):
        first, last = step == 0, step == ITERS - 1
        rows = lax.all_to_all(copies, PLANE, 0, 0)
        sums = summed(rows, column, [entries] if first else [])
        square = functools.partial(square_kernel, first, 2 * step)
        if first:
            outs = [tile, shape((CORES, *entry.shape), F32)]
            column, entries = call(square, [], [sums, place], outs)
        else:
            (column,) = call(square, [], [sums, place, entries], [tile])
        given = [summed(rows, column), place, entries, both]
        if last:
            (out,) = call(functools.partial(last_kernel, 2 * step + 1), [], given, [tile])
        else:
            update = functools.partial(update_kernel, 2 * step + 1)
            both, column, copies = call(update, [], given, [two_tiles, tile], copied)
    return out


def solution(mesh):
    spec = P("blk", PLANE)
    return jax.shard_map(
        on_device,
        mesh=mesh,
        in_specs=(spec, P(None, None, "blk", PLANE)),
        out_specs=spec,
        check_vma=False,
    )
```

time: 506 us -> 161 us (0.32)
  waiting for transfers between devices: 480 us -> 0.01 us
  blocking collectives: 0 us -> 143 us
  between operations: 13.5 us -> 0.08 us
  starting transfers between devices: 0.2 us -> 11.5 us
  matrix products: 9.36 us -> 0 us
  Pallas kernels: 0 us -> 5.38 us
    all_gather x6 -> x0, waiting for transfers between devices: 478 us -> none  [the longest x2 179 us: on_device(): row_slab = lax.all_gather(current, ('row', 'depth'), axis=1, tiled=True)]
    all_gather x0 -> x9, blocking collectives: none -> 143 us  [the longest x4 119 us: summed(): columns = lax.all_gather(column, 'blk', axis=0, axis_index_groups=rings)]
    all_to_all x0 -> x2, starting transfers between devices: none -> 11.5 us  [on_device(): rows = lax.all_to_all(copies, PLANE, 0, 0)]
    dot_general x4 -> x0, matrix products: 9.36 us -> none  [add_product(): return jnp.dot(row_slab, tile_in, preferred_element_type=jnp.float32)]
    pallas_call x0 -> x10, Pallas kernels: none -> 5.38 us  [call(): pl.pallas_call(kernel, out_shape=outs, in_specs=[pl.BlockSpec(memory_spac...]
  transfers between devices with their start and end apart: 6 -> 2, of which waited for: 6 -> 0; matrix products, arithmetic and copies ran while one was open for 0% -> 0% of each run, Pallas kernels for 0% -> 0%
where the time goes in v6:
time: 161 us
  blocking collectives  143 us (89%)
  starting transfers between devices  11.5 us (7%)
  Pallas kernels  5.38 us (3%)
    all_gather x4, blocking collectives, summed(): columns = lax.all_gather(column, 'blk', axis=0, axis_index_groups=rings)  119 us
    all_gather x5, blocking collectives, between_cores(): return lax.all_gather(value, 'blk', axis=0, axis_index_groups=pairs)  23.9 us
    all_to_all x2, starting transfers between devices, on_device(): rows = lax.all_to_all(copies, PLANE, 0, 0)  11.5 us
    pallas_call x10, Pallas kernels, call(): pl.pallas_call(kernel, out_shape=outs, in_specs=[pl.BlockSpec(memory_spac...  5.38 us
  transfers between devices with their start and end apart: 2, of which 0 were waited for; matrix products, arithmetic and copies ran while one was open for 0% of the time, Pallas kernels for 0%

profile of v6, /device:TPU:1, one launch (start us, length us, event | category | flops | bytes accessed | tf_op | source)
XLA Modules:
  0.0 161.1 jit_solution(10495424922692019305)
XLA Ops:
  0.0 0.0 copy-start
  0.0 0.7 copy-done
  0.7 0.6 shard_map.28
  1.3 15.9 %all-gather = bf16[256,128]{1,0:T(8,128)(2,1)S(1)} all-gather(bf16[128,128]{1,0:T(8,128)(2,1)} %param.2), channel_id=2, replica_groups={{0,32},{64,96},{128,160},{192,224},{256,288},{320,352},{384,416},{448,4..., dimensions={0}, use_global_device_ids=true | all-gather | bytes 98304 | tf_op jit(solution)/shard_map/all_gather | solution.py:194
  17.2 1.1 shard_map.29
  18.3 3.9 %all-to-all-start = ((bf16[32,128,128]{2,1,0:T(8,128)(2,1)}), bf16[32,128,128]{2,1,0:T(8,128)(2,1)S(1)}, u32[]{:S(2)}, u32[]{:S(2)}) async-start(bf16[32,128,128]{2,1,0:T(8,128)(2,1)} %get-tuple-element.21), calls=%async_computation | async-start | bytes 2097152 | tf_op jit(solution)/shard_map/all_to_all | solution.py:208
  22.3 36.5 %all-gather.1 = bf16[2048,128]{1,0:T(8,128)(2,1)S(1)} all-gather(bf16[128,128]{1,0:T(8,128)(2,1)S(1)} %get-tuple-element.22), channel_id=3, replica_groups={{0,96,128,224,256,352,384,480,512,608,640,736,768,864,896,992},{32,64,1..., dimensions={0}, use_global_device_ids=true | all-gather | bytes 557056 | tf_op jit(solution)/shard_map/all_gather | solution.py:197
  58.8 0.0 all-to-all-done.rows_ref
  58.8 0.4 shard_map.30
  59.3 2.0 %all-gather.2 = f32[544,128]{1,0:T(8,128)S(1)} all-gather(f32[272,128]{1,0:T(8,128)S(1)} %shard_map.30), channel_id=4, replica_groups={{0,32},{64,96},{128,160},{192,224},{256,288},{320,352},{384,416},{448,4..., dimensions={0}, use_global_device_ids=true | all-gather | bytes 417792 | tf_op jit(solution)/shard_map/all_gather | solution.py:194
  61.3 26.7 %all-gather.3 = bf16[2048,128]{1,0:T(8,128)(2,1)S(1)} all-gather(bf16[128,128]{1,0:T(8,128)(2,1)S(1)} %get-tuple-element.24), channel_id=5, replica_groups={{0,96,128,224,256,352,384,480,512,608,640,736,768,864,896,992},{32,64,1..., dimensions={0}, use_global_device_ids=true | all-gather | bytes 557056 | tf_op jit(solution)/shard_map/all_gather | solution.py:197
  88.1 0.4 shard_map.32
  88.5 2.0 %all-gather.4 = f32[512,128]{1,0:T(8,128)S(1)} all-gather(f32[256,128]{1,0:T(8,128)S(1)} %shard_map.32), channel_id=6, replica_groups={{0,32},{64,96},{128,160},{192,224},{256,288},{320,352},{384,416},{448,4..., dimensions={0}, use_global_device_ids=true | all-gather | bytes 393216 | tf_op jit(solution)/shard_map/all_gather | solution.py:194
  90.5 1.2 shard_map.33
  91.7 7.6 %all-to-all-start.1 = ((bf16[32,128,128]{2,1,0:T(8,128)(2,1)}), bf16[32,128,128]{2,1,0:T(8,128)(2,1)S(1)}, u32[]{:S(2)}, u32[]{:S(2)}) async-start(bf16[32,128,128]{2,1,0:T(8,128)(2,1)} %get-tuple-element.26), calls=%async_computation.1 | async-start | bytes 2097152 | tf_op jit(solution)/shard_map/all_to_all | solution.py:208
  99.3 29.3 %all-gather.5 = bf16[2048,128]{1,0:T(8,128)(2,1)S(1)} all-gather(bf16[128,128]{1,0:T(8,128)(2,1)S(1)} %get-tuple-element.27), channel_id=7, replica_groups={{0,96,128,224,256,352,384,480,512,608,640,736,768,864,896,992},{32,64,1..., dimensions={0}, use_global_device_ids=true | all-gather | bytes 557056 | tf_op jit(solution)/shard_map/all_gather | solution.py:197
  128.6 0.0 all-to-all-done.1.rows_ref
  128.6 0.4 shard_map.34
  129.0 2.0 %all-gather.6 = f32[512,128]{1,0:T(8,128)S(1)} all-gather(f32[256,128]{1,0:T(8,128)S(1)} %shard_map.34), channel_id=8, replica_groups={{0,32},{64,96},{128,160},{192,224},{256,288},{320,352},{384,416},{448,4..., dimensions={0}, use_global_device_ids=true | all-gather | bytes 393216 | tf_op jit(solution)/shard_map/all_gather | solution.py:194
  131.0 26.9 %all-gather.7 = bf16[2048,128]{1,0:T(8,128)(2,1)S(1)} all-gather(bf16[128,128]{1,0:T(8,128)(2,1)S(1)} %shard_map.35), channel_id=9, replica_groups={{0,96,128,224,256,352,384,480,512,608,640,736,768,864,896,992},{32,64,1..., dimensions={0}, use_global_device_ids=true | all-gather | bytes 557056 | tf_op jit(solution)/shard_map/all_gather | solution.py:197
  158.0 0.4 shard_map.36
  158.4 2.0 %all-gather.8 = f32[512,128]{1,0:T(8,128)S(1)} all-gather(f32[256,128]{1,0:T(8,128)S(1)} %shard_map.36), channel_id=10, replica_groups={{0,32},{64,96},{128,160},{192,224},{256,288},{320,352},{384,416},{448,4..., dimensions={0}, use_global_device_ids=true | all-gather | bytes 393216 | tf_op jit(solution)/shard_map/all_gather | solution.py:194
  160.4 0.7 shard_map.37
  (2 shorter events, 0.0 us)
Async XLA Ops:
  0.0 0.7 copy-start
  18.3 40.5 %all-to-all-start = ((bf16[32,128,128]{2,1,0:T(8,128)(2,1)}), bf16[32,128,128]{2,1,0:T(8,128)(2,1)S(1)}, u32[]{:S(2)}, u32[]{:S(2)}) async-start(bf16[32,128,128]{2,1,0:T(8,128)(2,1)} %get-tuple-element.21), calls=%async_computation | async-start | bytes 2097152 | tf_op jit(solution)/shard_map/all_to_all | solution.py:208
  91.7 36.9 %all-to-all-start.1 = ((bf16[32,128,128]{2,1,0:T(8,128)(2,1)}), bf16[32,128,128]{2,1,0:T(8,128)(2,1)S(1)}, u32[]{:S(2)}, u32[]{:S(2)}) async-start(bf16[32,128,128]{2,1,0:T(8,128)(2,1)} %get-tuple-element.26), calls=%async_computation.1 | async-start | bytes 2097152 | tf_op jit(solution)/shard_map/all_to_all | solution.py:208

commit v7 on v6

--- a/solution.py
+++ b/solution.py
@@ -20,10 +20,12 @@
     return lax.broadcasted_iota(jnp.int32, shape, len(shape) - 1)
 
 
-def pieces(values, place_ref):
+def pieces(values):
     side = values[0].shape[0]
     half = side // 2
-    ring, odd = place_ref[0:1, :] == 1, place_ref[1:2, :] == 1
+    blk = lax.axis_index("blk")
+    ring = jnp.full((1, side), (blk // CORES + blk) % CORES, jnp.int32) == 1
+    odd = jnp.full((1, side), lax.axis_index(PLANE) % CORES, jnp.int32) == 1
     first = jnp.where(odd, values[1], values[0])
     second = jnp.where(odd, values[0], values[1])
     left = jnp.where(ring, pltpu.roll(first, half, 1), first)
@@ -49,25 +51,9 @@
         copy.wait()
 
 
-def place_kernel(mask_ref, place_ref, entry_ref):
-    width = entry_ref.shape[1]
-    blk = lax.axis_index("blk")
-    ring = (blk // CORES + blk) % CORES
-    for i, value in enumerate((ring, lax.axis_index(PLANE) % CORES, blk % CORES)):
-        place_ref[i : i + 1, :] = jnp.full((1, width), value, jnp.int32)
-    row = 0
-    for step in range(mask_ref.shape[0]):
-        for which in range(mask_ref.shape[1]):
-            for i in range(mask_ref.shape[2]):
-                for j in range(mask_ref.shape[3]):
-                    value = mask_ref[step, which, i, j].astype(F32)
-                    entry_ref[row : row + 1, :] = jnp.full((1, width), value, F32)
-                    row += 1
-
-
-def first_kernel(both_ref, place_ref, column_ref, copies_ref, few_ref, sem):
+def first_kernel(both_ref, column_ref, copies_ref, few_ref, sem):
     values = [both_ref[i].astype(F32) for i in range(CORES)]
-    row_piece, column_piece = pieces(values, place_ref)
+    row_piece, column_piece = pieces(values)
     column_ref[...] = column_piece
     copy_out(row_piece, copies_ref, few_ref, sem)
 
@@ -114,18 +100,18 @@
 
 def square_kernel(first, number, sums_ref, *refs):
     if first:
-        place_ref, column_ref, entries_ref = refs
+        column_ref, entries_ref = refs
         side = column_ref.shape[0]
         for i in range(CORES):
             entries_ref[i] = sums_ref[i, CORES * side :, :]
     else:
-        place_ref, entries_ref, column_ref = refs
+        entries_ref, column_ref = refs
         side = column_ref.shape[0]
     values = []
     for i in range(CORES):
         at = slice(i * side, (i + 1) * side)
         values.append(filtered(sums_ref[0, at, :] + sums_ref[1, at, :], entries_ref[i], number))
-    column_ref[...] = pieces(values, place_ref)[1]
+    column_ref[...] = pieces(values)[1]
 
 
 def updated(number, sums_ref, entries_ref, both_ref):
@@ -140,19 +126,20 @@
 
 
 def update_kernel(
-    number, sums_ref, place_ref, entries_ref, both_ref, new_ref, column_ref, copies_ref, few_ref, sem
+    number, sums_ref, entries_ref, both_ref, new_ref, column_ref, copies_ref, few_ref, sem
 ):
     values = updated(number, sums_ref, entries_ref, both_ref)
     for i in range(CORES):
         new_ref[i] = values[i].astype(BF16)
-    row_piece, column_piece = pieces(values, place_ref)
+    row_piece, column_piece = pieces(values)
     column_ref[...] = column_piece
     copy_out(row_piece, copies_ref, few_ref, sem)
 
 
-def last_kernel(number, sums_ref, place_ref, entries_ref, both_ref, out_ref):
+def last_kernel(number, sums_ref, entries_ref, both_ref, out_ref):
     values = updated(number, sums_ref, entries_ref, both_ref)
-    out_ref[...] = jnp.where(place_ref[2:3, :] == 1, values[1], values[0]).astype(BF16)
+    core = jnp.full((1, out_ref.shape[1]), lax.axis_index("blk") % CORES, jnp.int32)
+    out_ref[...] = jnp.where(core == 1, values[1], values[0]).astype(BF16)
 
 
 def call(kernel, scalars, arrays, outs, copies=None):
@@ -199,10 +186,10 @@
         (partial,) = call(partial_kernel, [], [rows, columns, *more], [shape((height, cols), F32)])
         return between_cores(partial)
 
-    place, entries = call(place_kernel, [keep_mask], [], [shape((8, cols), jnp.int32), entry])
-    place, entries, x_start = lax.optimization_barrier((place, entries, x_start))
+    entries = jnp.broadcast_to(keep_mask.reshape(-1, 1), entry.shape).astype(F32)
+    entries, x_start = lax.optimization_barrier((entries, x_start))
     both = between_cores(x_start)
-    column, copies = call(first_kernel, [], [both, place], [tile], copied)
+    column, copies = call(first_kernel, [], [both], [tile], copied)
     for step in range(ITERS):
         first, last = step == 0, step == ITERS - 1
         rows = lax.all_to_all(copies, PLANE, 0, 0)
@@ -210,10 +197,10 @@
         square = functools.partial(square_kernel, first, 2 * step)
         if first:
             outs = [tile, shape((CORES, *entry.shape), F32)]
-            column, entries = call(square, [], [sums, place], outs)
+            column, entries = call(square, [], [sums], outs)
         else:
-            (column,) = call(square, [], [sums, place, entries], [tile])
-        given = [summed(rows, column), place, entries, both]
+            (column,) = call(square, [], [sums, entries], [tile])
+        given = [summed(rows, column), entries, both]
         if last:
             (out,) = call(functools.partial(last_kernel, 2 * step + 1), [], given, [tile])
         else:

time: 161 us -> 161 us (level)
    pallas_call x10 -> x9, Pallas kernels: 5.38 us -> 4.77 us  [call(): pl.pallas_call(kernel, out_shape=outs, in_specs=[pl.BlockSpec(memory_spac...]
where the time goes in v7:
time: 161 us
  blocking collectives  143 us (89%)
  starting transfers between devices  11.5 us (7%)
  Pallas kernels  4.77 us (3%)
    all_gather x4, blocking collectives, summed(): columns = lax.all_gather(column, 'blk', axis=0, axis_index_groups=rings)  119 us
    all_gather x5, blocking collectives, between_cores(): return lax.all_gather(value, 'blk', axis=0, axis_index_groups=pairs)  23.9 us
    all_to_all x2, starting transfers between devices, on_device(): rows = lax.all_to_all(copies, PLANE, 0, 0)  11.5 us
    pallas_call x9, Pallas kernels, call(): pl.pallas_call(kernel, out_shape=outs, in_specs=[pl.BlockSpec(memory_spac...  4.77 us
  transfers between devices with their start and end apart: 2, of which 0 were waited for; matrix products, arithmetic and copies ran while one was open for 0% of the time, Pallas kernels for 0%

profile of v7, /device:TPU:1, one launch (start us, length us, event | category | flops | bytes accessed | tf_op | source)
XLA Modules:
  0.0 160.6 jit_solution(12455635374161439095)
XLA Ops:
  0.0 0.7 convert_element_type.7
  0.7 0.1 convert_element_type.8
  0.8 0.1 broadcast_in_dim.2.refs_0_
  0.8 15.9 %all-gather = bf16[256,128]{1,0:T(8,128)(2,1)S(1)} all-gather(bf16[128,128]{1,0:T(8,128)(2,1)} %param.2), channel_id=2, replica_groups={{0,32},{64,96},{128,160},{192,224},{256,288},{320,352},{384,416},{448,4..., dimensions={0}, use_global_device_ids=true | all-gather | bytes 98304 | tf_op jit(solution)/shard_map/all_gather | solution.py:181
  16.7 1.1 shard_map.28
  17.9 3.9 %all-to-all-start = ((bf16[32,128,128]{2,1,0:T(8,128)(2,1)}), bf16[32,128,128]{2,1,0:T(8,128)(2,1)S(1)}, u32[]{:S(2)}, u32[]{:S(2)}) async-start(bf16[32,128,128]{2,1,0:T(8,128)(2,1)} %get-tuple-element.15), calls=%async_computation | async-start | bytes 2097152 | tf_op jit(solution)/shard_map/all_to_all | solution.py:195
  21.8 36.5 %all-gather.1 = bf16[2048,128]{1,0:T(8,128)(2,1)S(1)} all-gather(bf16[128,128]{1,0:T(8,128)(2,1)S(1)} %get-tuple-element.16), channel_id=3, replica_groups={{0,96,128,224,256,352,384,480,512,608,640,736,768,864,896,992},{32,64,1..., dimensions={0}, use_global_device_ids=true | all-gather | bytes 557056 | tf_op jit(solution)/shard_map/all_gather | solution.py:184
  58.3 0.0 all-to-all-done.rows_ref
  58.3 0.4 shard_map.29
  58.8 2.0 %all-gather.2 = f32[544,128]{1,0:T(8,128)S(1)} all-gather(f32[272,128]{1,0:T(8,128)S(1)} %shard_map.29), channel_id=4, replica_groups={{0,32},{64,96},{128,160},{192,224},{256,288},{320,352},{384,416},{448,4..., dimensions={0}, use_global_device_ids=true | all-gather | bytes 417792 | tf_op jit(solution)/shard_map/all_gather | solution.py:181
  60.9 26.7 %all-gather.3 = bf16[2048,128]{1,0:T(8,128)(2,1)S(1)} all-gather(bf16[128,128]{1,0:T(8,128)(2,1)S(1)} %get-tuple-element.18), channel_id=5, replica_groups={{0,96,128,224,256,352,384,480,512,608,640,736,768,864,896,992},{32,64,1..., dimensions={0}, use_global_device_ids=true | all-gather | bytes 557056 | tf_op jit(solution)/shard_map/all_gather | solution.py:184
  87.6 0.4 shard_map.31
  88.0 2.0 %all-gather.4 = f32[512,128]{1,0:T(8,128)S(1)} all-gather(f32[256,128]{1,0:T(8,128)S(1)} %shard_map.31), channel_id=6, replica_groups={{0,32},{64,96},{128,160},{192,224},{256,288},{320,352},{384,416},{448,4..., dimensions={0}, use_global_device_ids=true | all-gather | bytes 393216 | tf_op jit(solution)/shard_map/all_gather | solution.py:181
  90.0 1.2 shard_map.32
  91.2 7.6 %all-to-all-start.1 = ((bf16[32,128,128]{2,1,0:T(8,128)(2,1)}), bf16[32,128,128]{2,1,0:T(8,128)(2,1)S(1)}, u32[]{:S(2)}, u32[]{:S(2)}) async-start(bf16[32,128,128]{2,1,0:T(8,128)(2,1)} %get-tuple-element.20), calls=%async_computation.1 | async-start | bytes 2097152 | tf_op jit(solution)/shard_map/all_to_all | solution.py:195
  98.8 29.3 %all-gather.5 = bf16[2048,128]{1,0:T(8,128)(2,1)S(1)} all-gather(bf16[128,128]{1,0:T(8,128)(2,1)S(1)} %get-tuple-element.21), channel_id=7, replica_groups={{0,96,128,224,256,352,384,480,512,608,640,736,768,864,896,992},{32,64,1..., dimensions={0}, use_global_device_ids=true | all-gather | bytes 557056 | tf_op jit(solution)/shard_map/all_gather | solution.py:184
  128.1 0.0 all-to-all-done.1.rows_ref
  128.1 0.4 shard_map.33
  128.5 2.0 %all-gather.6 = f32[512,128]{1,0:T(8,128)S(1)} all-gather(f32[256,128]{1,0:T(8,128)S(1)} %shard_map.33), channel_id=8, replica_groups={{0,32},{64,96},{128,160},{192,224},{256,288},{320,352},{384,416},{448,4..., dimensions={0}, use_global_device_ids=true | all-gather | bytes 393216 | tf_op jit(solution)/shard_map/all_gather | solution.py:181
  130.6 26.9 %all-gather.7 = bf16[2048,128]{1,0:T(8,128)(2,1)S(1)} all-gather(bf16[128,128]{1,0:T(8,128)(2,1)S(1)} %shard_map.34), channel_id=9, replica_groups={{0,96,128,224,256,352,384,480,512,608,640,736,768,864,896,992},{32,64,1..., dimensions={0}, use_global_device_ids=true | all-gather | bytes 557056 | tf_op jit(solution)/shard_map/all_gather | solution.py:184
  157.5 0.4 shard_map.35
  158.0 2.0 %all-gather.8 = f32[512,128]{1,0:T(8,128)S(1)} all-gather(f32[256,128]{1,0:T(8,128)S(1)} %shard_map.35), channel_id=10, replica_groups={{0,32},{64,96},{128,160},{192,224},{256,288},{320,352},{384,416},{448,4..., dimensions={0}, use_global_device_ids=true | all-gather | bytes 393216 | tf_op jit(solution)/shard_map/all_gather | solution.py:181
  159.9 0.7 shard_map.36
  (2 shorter events, 0.0 us)
Async XLA Ops:
  17.9 40.5 %all-to-all-start = ((bf16[32,128,128]{2,1,0:T(8,128)(2,1)}), bf16[32,128,128]{2,1,0:T(8,128)(2,1)S(1)}, u32[]{:S(2)}, u32[]{:S(2)}) async-start(bf16[32,128,128]{2,1,0:T(8,128)(2,1)} %get-tuple-element.15), calls=%async_computation | async-start | bytes 2097152 | tf_op jit(solution)/shard_map/all_to_all | solution.py:195
  91.2 36.9 %all-to-all-start.1 = ((bf16[32,128,128]{2,1,0:T(8,128)(2,1)}), bf16[32,128,128]{2,1,0:T(8,128)(2,1)S(1)}, u32[]{:S(2)}, u32[]{:S(2)}) async-start(bf16[32,128,128]{2,1,0:T(8,128)(2,1)} %get-tuple-element.20), calls=%async_computation.1 | async-start | bytes 2097152 | tf_op jit(solution)/shard_map/all_to_all | solution.py:195

commit v8 on v7

--- a/solution.py
+++ b/solution.py
@@ -136,10 +136,18 @@
     copy_out(row_piece, copies_ref, few_ref, sem)
 
 
-def last_kernel(number, sums_ref, entries_ref, both_ref, out_ref):
-    values = updated(number, sums_ref, entries_ref, both_ref)
-    core = jnp.full((1, out_ref.shape[1]), lax.axis_index("blk") % CORES, jnp.int32)
-    out_ref[...] = jnp.where(core == 1, values[1], values[0]).astype(BF16)
+def last_partial_kernel(rows_ref, columns_ref, sent_ref, kept_ref):
+    value = partial_sums(rows_ref, columns_ref)
+    core = jnp.full((1, sent_ref.shape[1]), lax.axis_index("blk") % CORES, jnp.int32) == 1
+    sent_ref[...] = jnp.where(core, value[0], value[1])
+    kept_ref[...] = jnp.where(core, value[1], value[0])
+
+
+def last_kernel(number, sent_ref, kept_ref, entries_ref, both_ref, out_ref):
+    core = lax.axis_index("blk") % CORES
+    cube_term = kept_ref[...] + sent_ref[1 - core]
+    value = 1.5 * both_ref[core].astype(F32) - 0.5 * cube_term
+    out_ref[...] = filtered(value, entries_ref[core], number).astype(BF16)
 
 
 def call(kernel, scalars, arrays, outs, copies=None):
@@ -200,10 +208,14 @@
             column, entries = call(square, [], [sums], outs)
         else:
             (column,) = call(square, [], [sums, entries], [tile])
-        given = [summed(rows, column), entries, both]
         if last:
+            columns = lax.all_gather(column, "blk", axis=0, axis_index_groups=rings)
+            sums = [shape((side, cols), F32)] * CORES
+            sent, kept = call(last_partial_kernel, [], [rows, columns], sums)
+            given = [between_cores(sent), kept, entries, both]
             (out,) = call(functools.partial(last_kernel, 2 * step + 1), [], given, [tile])
         else:
+            given = [summed(rows, column), entries, both]
             update = functools.partial(update_kernel, 2 * step + 1)
             both, column, copies = call(update, [], given, [two_tiles, tile], copied)
     return out

time: 161 us -> 161 us (level)
    all_gather x4 -> x3, blocking collectives: 119 us -> 92.5 us  [summed(): columns = lax.all_gather(column, 'blk', axis=0, axis_index_groups=rings)]
    all_gather x0 -> x1, blocking collectives: none -> 26.9 us  [on_device(): columns = lax.all_gather(column, 'blk', axis=0, axis_index_groups=rings)]
where the time goes in v8:
time: 161 us; the launch traced here: 160 us
  blocking collectives  143 us (89%)
  starting transfers between devices  11.5 us (7%)
  Pallas kernels  4.76 us (3%)
    all_gather x3, blocking collectives, summed(): columns = lax.all_gather(column, 'blk', axis=0, axis_index_groups=rings)  92.5 us
    all_gather x1, blocking collectives, on_device(): columns = lax.all_gather(column, 'blk', axis=0, axis_index_groups=rings)  26.9 us
    all_gather x5, blocking collectives, between_cores(): return lax.all_gather(value, 'blk', axis=0, axis_index_groups=pairs)  23.8 us
    all_to_all x2, starting transfers between devices, on_device(): rows = lax.all_to_all(copies, PLANE, 0, 0)  11.5 us
    pallas_call x9, Pallas kernels, call(): pl.pallas_call(kernel, out_shape=outs, in_specs=[pl.BlockSpec(memory_spac...  4.76 us
  transfers between devices with their start and end apart: 2, of which 0 were waited for; matrix products, arithmetic and copies ran while one was open for 0% of the time, Pallas kernels for 0%

profile of v8, /device:TPU:1, one launch (start us, length us, event | category | flops | bytes accessed | tf_op | source)
XLA Modules:
  0.0 160.5 jit_solution(1533208203861966473)
XLA Ops:
  0.0 0.7 convert_element_type.7
  0.7 0.1 convert_element_type.8
  0.8 0.1 broadcast_in_dim.2.refs_0_
  0.8 15.9 %all-gather = bf16[256,128]{1,0:T(8,128)(2,1)S(1)} all-gather(bf16[128,128]{1,0:T(8,128)(2,1)} %param.2), channel_id=2, replica_groups={{0,32},{64,96},{128,160},{192,224},{256,288},{320,352},{384,416},{448,4..., dimensions={0}, use_global_device_ids=true | all-gather | bytes 98304 | tf_op jit(solution)/shard_map/all_gather | solution.py:189
  16.7 1.1 shard_map.28
  17.9 3.9 %all-to-all-start = ((bf16[32,128,128]{2,1,0:T(8,128)(2,1)}), bf16[32,128,128]{2,1,0:T(8,128)(2,1)S(1)}, u32[]{:S(2)}, u32[]{:S(2)}) async-start(bf16[32,128,128]{2,1,0:T(8,128)(2,1)} %get-tuple-element.17), calls=%async_computation | async-start | bytes 2097152 | tf_op jit(solution)/shard_map/all_to_all | solution.py:203
  21.8 36.5 %all-gather.1 = bf16[2048,128]{1,0:T(8,128)(2,1)S(1)} all-gather(bf16[128,128]{1,0:T(8,128)(2,1)S(1)} %get-tuple-element.18), channel_id=3, replica_groups={{0,96,128,224,256,352,384,480,512,608,640,736,768,864,896,992},{32,64,1..., dimensions={0}, use_global_device_ids=true | all-gather | bytes 557056 | tf_op jit(solution)/shard_map/all_gather | solution.py:192
  58.3 0.0 all-to-all-done.rows_ref
  58.3 0.4 shard_map.29
  58.8 2.0 %all-gather.2 = f32[544,128]{1,0:T(8,128)S(1)} all-gather(f32[272,128]{1,0:T(8,128)S(1)} %shard_map.29), channel_id=4, replica_groups={{0,32},{64,96},{128,160},{192,224},{256,288},{320,352},{384,416},{448,4..., dimensions={0}, use_global_device_ids=true | all-gather | bytes 417792 | tf_op jit(solution)/shard_map/all_gather | solution.py:189
  60.9 26.7 %all-gather.3 = bf16[2048,128]{1,0:T(8,128)(2,1)S(1)} all-gather(bf16[128,128]{1,0:T(8,128)(2,1)S(1)} %get-tuple-element.20), channel_id=5, replica_groups={{0,96,128,224,256,352,384,480,512,608,640,736,768,864,896,992},{32,64,1..., dimensions={0}, use_global_device_ids=true | all-gather | bytes 557056 | tf_op jit(solution)/shard_map/all_gather | solution.py:192
  87.6 0.4 shard_map.31
  88.0 2.0 %all-gather.4 = f32[512,128]{1,0:T(8,128)S(1)} all-gather(f32[256,128]{1,0:T(8,128)S(1)} %shard_map.31), channel_id=6, replica_groups={{0,32},{64,96},{128,160},{192,224},{256,288},{320,352},{384,416},{448,4..., dimensions={0}, use_global_device_ids=true | all-gather | bytes 393216 | tf_op jit(solution)/shard_map/all_gather | solution.py:189
  90.0 1.2 shard_map.32
  91.2 7.6 %all-to-all-start.1 = ((bf16[32,128,128]{2,1,0:T(8,128)(2,1)}), bf16[32,128,128]{2,1,0:T(8,128)(2,1)S(1)}, u32[]{:S(2)}, u32[]{:S(2)}) async-start(bf16[32,128,128]{2,1,0:T(8,128)(2,1)} %get-tuple-element.22), calls=%async_computation.1 | async-start | bytes 2097152 | tf_op jit(solution)/shard_map/all_to_all | solution.py:203
  98.8 29.3 %all-gather.5 = bf16[2048,128]{1,0:T(8,128)(2,1)S(1)} all-gather(bf16[128,128]{1,0:T(8,128)(2,1)S(1)} %get-tuple-element.23), channel_id=7, replica_groups={{0,96,128,224,256,352,384,480,512,608,640,736,768,864,896,992},{32,64,1..., dimensions={0}, use_global_device_ids=true | all-gather | bytes 557056 | tf_op jit(solution)/shard_map/all_gather | solution.py:192
  128.1 0.0 all-to-all-done.1.rows_ref
  128.1 0.4 shard_map.33
  128.5 2.0 %all-gather.6 = f32[512,128]{1,0:T(8,128)S(1)} all-gather(f32[256,128]{1,0:T(8,128)S(1)} %shard_map.33), channel_id=8, replica_groups={{0,32},{64,96},{128,160},{192,224},{256,288},{320,352},{384,416},{448,4..., dimensions={0}, use_global_device_ids=true | all-gather | bytes 393216 | tf_op jit(solution)/shard_map/all_gather | solution.py:189
  130.5 26.9 %all-gather.7 = bf16[2048,128]{1,0:T(8,128)(2,1)S(1)} all-gather(bf16[128,128]{1,0:T(8,128)(2,1)S(1)} %shard_map.34), channel_id=9, replica_groups={{0,96,128,224,256,352,384,480,512,608,640,736,768,864,896,992},{32,64,1..., dimensions={0}, use_global_device_ids=true | all-gather | bytes 557056 | tf_op jit(solution)/shard_map/all_gather | solution.py:212
  157.5 0.4 shard_map.35
  157.9 1.9 %all-gather.8 = f32[256,128]{1,0:T(8,128)S(1)} all-gather(f32[128,128]{1,0:T(8,128)S(1)} %get-tuple-element.24), channel_id=10, replica_groups={{0,32},{64,96},{128,160},{192,224},{256,288},{320,352},{384,416},{448,4..., dimensions={0}, use_global_device_ids=true | all-gather | bytes 196608 | tf_op jit(solution)/shard_map/all_gather | solution.py:189
  159.8 0.6 shard_map.36
  (2 shorter events, 0.0 us)
Async XLA Ops:
  17.9 40.5 %all-to-all-start = ((bf16[32,128,128]{2,1,0:T(8,128)(2,1)}), bf16[32,128,128]{2,1,0:T(8,128)(2,1)S(1)}, u32[]{:S(2)}, u32[]{:S(2)}) async-start(bf16[32,128,128]{2,1,0:T(8,128)(2,1)} %get-tuple-element.17), calls=%async_computation | async-start | bytes 2097152 | tf_op jit(solution)/shard_map/all_to_all | solution.py:203
  91.2 36.9 %all-to-all-start.1 = ((bf16[32,128,128]{2,1,0:T(8,128)(2,1)}), bf16[32,128,128]{2,1,0:T(8,128)(2,1)S(1)}, u32[]{:S(2)}, u32[]{:S(2)}) async-start(bf16[32,128,128]{2,1,0:T(8,128)(2,1)} %get-tuple-element.22), calls=%async_computation.1 | async-start | bytes 2097152 | tf_op jit(solution)/shard_map/all_to_all | solution.py:203

commit v9 on v7

--- a/solution.py
+++ b/solution.py
@@ -107,11 +107,23 @@
     else:
         entries_ref, column_ref = refs
         side = column_ref.shape[0]
-    values = []
+    half = side // 2
+    blk = lax.axis_index("blk")
+    ring = (blk // CORES + blk) % CORES
+    low = lanes((1, column_ref.shape[1])) < BS
+    upper = jnp.full((1, column_ref.shape[1]), ring, jnp.int32) == 1
+    each = side // BS
     for i in range(CORES):
-        at = slice(i * side, (i + 1) * side)
-        values.append(filtered(sums_ref[0, at, :] + sums_ref[1, at, :], entries_ref[i], number))
-    column_ref[...] = pieces(values)[1]
+        at = pl.ds(pl.multiple_of(i * side + ring * half, half), half)
+        value = sums_ref[0, at, :] + sums_ref[1, at, :]
+        rows = []
+        for j in range(each):
+            row = (number * each + j) * each
+            left, right = entries_ref[i, row : row + 1, :], entries_ref[i, row + 1 : row + 2, :]
+            rows.append(jnp.where(low, left, right))
+        keep = jnp.where(upper, rows[1], rows[0])
+        value = jnp.where(keep == 1.0, value, 0.0)
+        column_ref[i * half : (i + 1) * half, :] = value.astype(BF16)
 
 
 def updated(number, sums_ref, entries_ref, both_ref):

time: 161 us -> 161 us (level)
  no operation moved by 1% of the time
where the time goes in v9:
time: 161 us
  blocking collectives  143 us (89%)
  starting transfers between devices  11.5 us (7%)
  Pallas kernels  4.75 us (3%)
    all_gather x4, blocking collectives, summed(): columns = lax.all_gather(column, 'blk', axis=0, axis_index_groups=rings)  119 us
    all_gather x5, blocking collectives, between_cores(): return lax.all_gather(value, 'blk', axis=0, axis_index_groups=pairs)  23.9 us
    all_to_all x2, starting transfers between devices, on_device(): rows = lax.all_to_all(copies, PLANE, 0, 0)  11.5 us
    pallas_call x9, Pallas kernels, call(): pl.pallas_call(kernel, out_shape=outs, in_specs=[pl.BlockSpec(memory_spac...  4.75 us
  transfers between devices with their start and end apart: 2, of which 0 were waited for; matrix products, arithmetic and copies ran while one was open for 0% of the time, Pallas kernels for 0%

profile of v9, /device:TPU:1, one launch (start us, length us, event | category | flops | bytes accessed | tf_op | source)
XLA Modules:
  0.0 160.6 jit_solution(13321804129898574558)
XLA Ops:
  0.0 0.7 convert_element_type.7
  0.7 0.1 convert_element_type.8
  0.8 0.1 broadcast_in_dim.2.refs_0_
  0.8 15.9 %all-gather = bf16[256,128]{1,0:T(8,128)(2,1)S(1)} all-gather(bf16[128,128]{1,0:T(8,128)(2,1)} %param.2), channel_id=2, replica_groups={{0,32},{64,96},{128,160},{192,224},{256,288},{320,352},{384,416},{448,4..., dimensions={0}, use_global_device_ids=true | all-gather | bytes 98304 | tf_op jit(solution)/shard_map/all_gather | solution.py:193
  16.7 1.1 shard_map.28
  17.9 3.9 %all-to-all-start = ((bf16[32,128,128]{2,1,0:T(8,128)(2,1)}), bf16[32,128,128]{2,1,0:T(8,128)(2,1)S(1)}, u32[]{:S(2)}, u32[]{:S(2)}) async-start(bf16[32,128,128]{2,1,0:T(8,128)(2,1)} %get-tuple-element.15), calls=%async_computation | async-start | bytes 2097152 | tf_op jit(solution)/shard_map/all_to_all | solution.py:207
  21.8 36.5 %all-gather.1 = bf16[2048,128]{1,0:T(8,128)(2,1)S(1)} all-gather(bf16[128,128]{1,0:T(8,128)(2,1)S(1)} %get-tuple-element.16), channel_id=3, replica_groups={{0,96,128,224,256,352,384,480,512,608,640,736,768,864,896,992},{32,64,1..., dimensions={0}, use_global_device_ids=true | all-gather | bytes 557056 | tf_op jit(solution)/shard_map/all_gather | solution.py:196
  58.3 0.0 all-to-all-done.rows_ref
  58.3 0.4 shard_map.29
  58.8 2.0 %all-gather.2 = f32[544,128]{1,0:T(8,128)S(1)} all-gather(f32[272,128]{1,0:T(8,128)S(1)} %shard_map.29), channel_id=4, replica_groups={{0,32},{64,96},{128,160},{192,224},{256,288},{320,352},{384,416},{448,4..., dimensions={0}, use_global_device_ids=true | all-gather | bytes 417792 | tf_op jit(solution)/shard_map/all_gather | solution.py:193
  60.9 26.7 %all-gather.3 = bf16[2048,128]{1,0:T(8,128)(2,1)S(1)} all-gather(bf16[128,128]{1,0:T(8,128)(2,1)S(1)} %get-tuple-element.18), channel_id=5, replica_groups={{0,96,128,224,256,352,384,480,512,608,640,736,768,864,896,992},{32,64,1..., dimensions={0}, use_global_device_ids=true | all-gather | bytes 557056 | tf_op jit(solution)/shard_map/all_gather | solution.py:196
  87.6 0.4 shard_map.31
  88.0 2.0 %all-gather.4 = f32[512,128]{1,0:T(8,128)S(1)} all-gather(f32[256,128]{1,0:T(8,128)S(1)} %shard_map.31), channel_id=6, replica_groups={{0,32},{64,96},{128,160},{192,224},{256,288},{320,352},{384,416},{448,4..., dimensions={0}, use_global_device_ids=true | all-gather | bytes 393216 | tf_op jit(solution)/shard_map/all_gather | solution.py:193
  90.0 1.2 shard_map.32
  91.2 7.6 %all-to-all-start.1 = ((bf16[32,128,128]{2,1,0:T(8,128)(2,1)}), bf16[32,128,128]{2,1,0:T(8,128)(2,1)S(1)}, u32[]{:S(2)}, u32[]{:S(2)}) async-start(bf16[32,128,128]{2,1,0:T(8,128)(2,1)} %get-tuple-element.20), calls=%async_computation.1 | async-start | bytes 2097152 | tf_op jit(solution)/shard_map/all_to_all | solution.py:207
  98.8 29.3 %all-gather.5 = bf16[2048,128]{1,0:T(8,128)(2,1)S(1)} all-gather(bf16[128,128]{1,0:T(8,128)(2,1)S(1)} %get-tuple-element.21), channel_id=7, replica_groups={{0,96,128,224,256,352,384,480,512,608,640,736,768,864,896,992},{32,64,1..., dimensions={0}, use_global_device_ids=true | all-gather | bytes 557056 | tf_op jit(solution)/shard_map/all_gather | solution.py:196
  128.1 0.0 all-to-all-done.1.rows_ref
  128.1 0.4 shard_map.33
  128.5 2.0 %all-gather.6 = f32[512,128]{1,0:T(8,128)S(1)} all-gather(f32[256,128]{1,0:T(8,128)S(1)} %shard_map.33), channel_id=8, replica_groups={{0,32},{64,96},{128,160},{192,224},{256,288},{320,352},{384,416},{448,4..., dimensions={0}, use_global_device_ids=true | all-gather | bytes 393216 | tf_op jit(solution)/shard_map/all_gather | solution.py:193
  130.5 26.9 %all-gather.7 = bf16[2048,128]{1,0:T(8,128)(2,1)S(1)} all-gather(bf16[128,128]{1,0:T(8,128)(2,1)S(1)} %shard_map.34), channel_id=9, replica_groups={{0,96,128,224,256,352,384,480,512,608,640,736,768,864,896,992},{32,64,1..., dimensions={0}, use_global_device_ids=true | all-gather | bytes 557056 | tf_op jit(solution)/shard_map/all_gather | solution.py:196
  157.5 0.4 shard_map.35
  157.9 2.0 %all-gather.8 = f32[512,128]{1,0:T(8,128)S(1)} all-gather(f32[256,128]{1,0:T(8,128)S(1)} %shard_map.35), channel_id=10, replica_groups={{0,32},{64,96},{128,160},{192,224},{256,288},{320,352},{384,416},{448,4..., dimensions={0}, use_global_device_ids=true | all-gather | bytes 393216 | tf_op jit(solution)/shard_map/all_gather | solution.py:193
  159.9 0.7 shard_map.36
  (2 shorter events, 0.0 us)
Async XLA Ops:
  17.9 40.5 %all-to-all-start = ((bf16[32,128,128]{2,1,0:T(8,128)(2,1)}), bf16[32,128,128]{2,1,0:T(8,128)(2,1)S(1)}, u32[]{:S(2)}, u32[]{:S(2)}) async-start(bf16[32,128,128]{2,1,0:T(8,128)(2,1)} %get-tuple-element.15), calls=%async_computation | async-start | bytes 2097152 | tf_op jit(solution)/shard_map/all_to_all | solution.py:207
  91.2 36.9 %all-to-all-start.1 = ((bf16[32,128,128]{2,1,0:T(8,128)(2,1)}), bf16[32,128,128]{2,1,0:T(8,128)(2,1)S(1)}, u32[]{:S(2)}, u32[]{:S(2)}) async-start(bf16[32,128,128]{2,1,0:T(8,128)(2,1)} %get-tuple-element.20), calls=%async_computation.1 | async-start | bytes 2097152 | tf_op jit(solution)/shard_map/all_to_all | solution.py:207
